TPU v7x, 32 devices: a whole 2x2x4 slice. The times are simulated.
32 devices in a mesh: dp: 8 (over y, x, core), tensor: 4 (over z).
Axes of the slice: x: 2, y: 2, z: 4, core: 2. Of those that a mesh axis runs over, the one named last changes fastest.
Arguments:
- gen_tokens: bfloat16 [24, 5, 256, 512], P('dp', None, 'tensor'), may hold values from -6 to 6
- rec_grad: bfloat16 [24, 5, 256, 512], P('dp', None, 'tensor'), may hold values from -6 to 6
- adv_grad: bfloat16 [24, 5, 256, 512], P('dp', None, 'tensor'), may hold values from -6 to 6
- gen_aspect: int32 [24], P('dp'), may hold values from 0 to 2
- gen_frames: int32 [24], P('dp'), may hold values from 1 to 5, 90 in all
- disc_tokens: bfloat16 [24, 5, 256, 512], P('dp', None, 'tensor'), may hold values from -6 to 6
- disc_aspect: int32 [24], P('dp'), may hold values from 0 to 2
- disc_frames: int32 [24], P('dp'), may hold values from 1 to 5, 90 in all
- disc_labels: int32 [24], P('dp'), may hold values from 0 to 1
- logit_gain: float32 [512], replicated, may hold values from 0.1 to 1.9
- adv_weight: float32 [1], replicated, may hold values from 0.5 to 1.5
- train_step: int32 [1], replicated, may hold values from 1000 to 19999
- ln1_gain: float32 [512], replicated, may hold values from 0.1 to 1.9
- ln1_bias: float32 [512], replicated, may hold values from -1.5 to 1.5
- spatial_qkv: bfloat16 [3, 512, 512], P(None, None, 'tensor'), may hold values from -0.25 to 0.25
- spatial_out: bfloat16 [512, 512], P('tensor'), may hold values from -0.75 to 0.75
- ln2_gain: float32 [512], replicated, may hold values from 0.1 to 1.9
- ln2_bias: float32 [512], replicated, may hold values from -1.5 to 1.5
- temporal_qkv: bfloat16 [3, 512, 512], P(None, None, 'tensor'), may hold values from -0.25 to 0.25
- temporal_out: bfloat16 [512, 512], P('tensor'), may hold values from -0.5 to 0.5
- ln3_gain: float32 [512], replicated, may hold values from 0.1 to 1.9
- ln3_bias: float32 [512], replicated, may hold values from -1.5 to 1.5
- mlp_in: bfloat16 [512, 2048], P(None, 'tensor'), may hold values from -0.25 to 0.25
- mlp_out: bfloat16 [2048, 512], P('tensor'), may hold values from -0.125 to 0.125
Outputs:
- gen_out: bfloat16 [24, 5, 256, 512], P('dp', None, 'tensor')
- gen_in_grad: bfloat16 [24, 5, 256, 512], P('dp', None, 'tensor')
- disc_out: bfloat16 [24, 5, 256, 512], P('dp', None, 'tensor')
- disc_in_grad: bfloat16 [24, 5, 256, 512], P('dp', None, 'tensor')
- ln1_gain_grad: float32 [512], P('dp')
- ln1_bias_grad: float32 [512], P('dp')
- spatial_qkv_grad: float32 [3, 512, 512], P(None, 'dp', 'tensor')
- spatial_out_grad: float32 [512, 512], P('tensor', 'dp')
- ln2_gain_grad: float32 [512], P('dp')
- ln2_bias_grad: float32 [512], P('dp')
- temporal_qkv_grad: float32 [3, 512, 512], P(None, 'dp', 'tensor')
- temporal_out_grad: float32 [512, 512], P('tensor', 'dp')
- ln3_gain_grad: float32 [512], P('dp')
- ln3_bias_grad: float32 [512], P('dp')
- mlp_in_grad: float32 [512, 2048], P('dp', 'tensor')
- mlp_out_grad: float32 [2048, 512], P('tensor', 'dp')
Inputs may be any that keep to these rules, and one draw needn't show every extreme that they name: `gen_aspect`: 0 lays a frame's patches on a square grid, 1 on a grid twice as wide, 2 on a grid half as wide; windows are 8 x 8 patches. `disc_aspect`: as gen_aspect. `gen_frames`: frames at or beyond a clip's count are padding; some clip has 5. `disc_frames`: as gen_frames.
All inputs are finite; a program needn't handle non-finite values. No bound on the sum of `gen_frames` or of `disc_frames` on one device may be relied on, other than what follows from the above.
Results may differ from a plain program's by a relative error of at most 0.025.
Values may be sent and summed in bfloat16 or wider, within the bound.
No kernel may reach another device: no remote copies, remote signals or barrier semaphores. Data moves between devices by JAX's collectives and lax.ppermute only.
A program may use at most 320 MiB of HBM per device.

v0:
```python
from functools import partial
import math

import jax
import jax.numpy as jnp
from jax import lax
from jax.sharding import PartitionSpec as P

HEAD_DIM = 64
P_SIZE = 256
WIN = 8
HALF = 5000


EPS = 1e-05


def layer_norm(value, norm_gain, norm_bias):
    average = jnp.mean(value, axis=-1, keepdims=True)
    centred = value - average
    variance = jnp.mean(centred * centred, axis=-1, keepdims=True)
    return centred * lax.rsqrt(variance + EPS) * norm_gain + norm_bias


def gelu_exact(values):
    return jax.nn.gelu(values, approximate=False)


def pack_rows(arrays, dims, count):
    pieces = []
    shapes = []
    for array, dim in zip(arrays, dims):
        moved = jnp.moveaxis(array, dim, 0)
        shapes.append(moved.shape)
        pieces.append(moved.reshape(count, -1))
    return (jnp.concatenate(pieces, axis=1), shapes)


def unpack_rows(flat, shapes, dims, count):
    results = []
    offset = 0
    for shape, dim in zip(shapes, dims):
        width = math.prod(shape) // count
        piece = flat[0, offset : offset + width].reshape((shape[0] // count,) + tuple(shape[1:]))
        results.append(jnp.moveaxis(piece, 0, dim))
        offset = offset + width
    return tuple(results)


def window_maps(aspect, tokens_frame):
    grid_side = math.isqrt(tokens_frame)
    window_area = WIN * WIN
    grid_width = jnp.where(
        aspect == 1, 2 * grid_side, jnp.where(aspect == 2, grid_side // 2, grid_side)
    ).astype(jnp.int32)[:, None]
    across = grid_width // WIN
    places = jnp.arange(tokens_frame, dtype=jnp.int32)[None, :]
    window = places // window_area
    inside = places % window_area
    grid_row = window // across * WIN + inside // WIN
    grid_col = window % across * WIN + inside % WIN
    forward_order = grid_row * grid_width + grid_col
    raster_row = places // grid_width
    raster_col = places % grid_width
    back_order = (
        (raster_row // WIN * across + raster_col // WIN) * window_area
        + raster_row % WIN * WIN
        + raster_col % WIN
    )
    return (forward_order, back_order)


def reorder(values, order):
    return jax.vmap(partial(jnp.take, axis=1))(values, order)


def spatial_groups(win_order, values):
    reordered = reorder(values, win_order)
    return reordered.reshape(-1, WIN * WIN, values.shape[-1] // HEAD_DIM, HEAD_DIM)


def spatial_merge(win_back, full_shape, values):
    return reorder(values.reshape(full_shape), win_back)


def temporal_groups(values):
    clip_count, frame_count, places, columns = values.shape
    heads_split = values.reshape(clip_count, frame_count, places, columns // HEAD_DIM, HEAD_DIM)
    moved = jnp.transpose(heads_split, (0, 2, 1, 3, 4))
    return moved.reshape(clip_count * places, frame_count, columns // HEAD_DIM, HEAD_DIM)


def temporal_merge(full_shape, values):
    clip_count, frame_count, places, columns = full_shape
    heads_split = values.reshape(clip_count, places, frame_count, columns // HEAD_DIM, HEAD_DIM)
    return jnp.transpose(heads_split, (0, 2, 1, 3, 4)).reshape(full_shape)


def gather_rows(normed):
    return lax.all_gather(normed, "tensor", axis=2, tiled=True)


def scatter_rows(partial_out):
    return lax.psum_scatter(
        partial_out.astype(jnp.bfloat16), "tensor", scatter_dimension=2, tiled=True
    ).astype(jnp.float32)


def gather_grads(grad_low):
    return lax.all_gather(grad_low, "tensor", axis=2, tiled=True)


def scatter_grads(partial_grad):
    return lax.psum_scatter(
        partial_grad.astype(jnp.bfloat16), "tensor", scatter_dimension=2, tiled=True
    ).astype(jnp.float32)


def input_weight_grad(normed, grad_rows, pattern, zero_init):
    shard_rows = lax.all_gather(normed, "tensor", axis=2, tiled=True)
    matching = lax.slice_in_dim(grad_rows, 0, shard_rows.shape[2], axis=grad_rows.ndim - 2)
    return zero_init + jnp.einsum(pattern, shard_rows, matching, preferred_element_type=jnp.float32)


def score_block(queries, key_rows, allowed):
    scores = jnp.einsum(
        "bqhd,bkhd->bhqk", queries, key_rows, preferred_element_type=jnp.float32
    ) * (1.0 / math.sqrt(HEAD_DIM))
    if allowed is not None:
        scores = jnp.where(allowed, scores, -1e30)
    return scores


def attend(queries, key_rows, value_rows, allowed):
    scores = score_block(queries, key_rows, allowed)
    log_total = jax.scipy.special.logsumexp(scores, axis=-1, keepdims=True)
    prob_low = jnp.exp(scores - log_total).astype(jnp.bfloat16)
    attended = jnp.einsum(
        "bhqk,bkhd->bqhd", prob_low, value_rows, preferred_element_type=jnp.float32
    ).astype(jnp.bfloat16)
    return (attended, log_total)


def attend_grad(grad_att, queries, key_rows, value_rows, log_total, allowed):
    score_scale = 1.0 / math.sqrt(HEAD_DIM)
    prob_full = jnp.exp(score_block(queries, key_rows, allowed) - log_total)
    grad_values = jnp.einsum(
        "bhqk,bqhd->bkhd",
        prob_full.astype(jnp.bfloat16),
        grad_att,
        preferred_element_type=jnp.float32,
    ).astype(jnp.bfloat16)
    grad_prob = jnp.einsum(
        "bqhd,bkhd->bhqk", grad_att, value_rows, preferred_element_type=jnp.float32
    )
    grad_scores = (
        prob_full * (grad_prob - jnp.sum(prob_full * grad_prob, axis=-1, keepdims=True))
    ).astype(jnp.bfloat16)
    grad_queries = (
        jnp.einsum("bhqk,bkhd->bqhd", grad_scores, key_rows, preferred_element_type=jnp.float32)
        * score_scale
    ).astype(jnp.bfloat16)
    grad_keys = (
        jnp.einsum("bhqk,bqhd->bkhd", grad_scores, queries, preferred_element_type=jnp.float32)
        * score_scale
    ).astype(jnp.bfloat16)
    return (grad_queries, grad_keys, grad_values)


def attention_forward(residual, norm_gain, norm_bias, w_qkv, w_out, grouping, merging, allowed):
    normed = layer_norm(residual, norm_gain, norm_bias).astype(jnp.bfloat16)
    gathered = gather_rows(normed)
    packed = jnp.einsum(
        "cfpd,kde->kcfpe", gathered, w_qkv, preferred_element_type=jnp.float32
    ).astype(jnp.bfloat16)
    queries, key_rows, value_rows = (grouping(packed[0]), grouping(packed[1]), grouping(packed[2]))
    attended, log_total = attend(queries, key_rows, value_rows, allowed)
    merged = merging(attended)
    partial_out = jnp.einsum("cfpe,ed->cfpd", merged, w_out, preferred_element_type=jnp.float32)
    updated = residual + scatter_rows(partial_out)
    return (updated, (normed, gathered, queries, key_rows, value_rows, log_total, merged))


def attention_backward(
    grad_out, residual, norm_gain, norm_bias, w_qkv, w_out, grouping, merging, allowed, saved
):
    normed, gathered, queries, key_rows, value_rows, log_total, merged = saved
    grad_branch = gather_grads(grad_out.astype(jnp.bfloat16))
    grad_wout = jnp.einsum("cfpe,cfpd->ed", merged, grad_branch, preferred_element_type=jnp.float32)
    grad_merged = jnp.einsum(
        "cfpd,ed->cfpe", grad_branch, w_out, preferred_element_type=jnp.float32
    ).astype(jnp.bfloat16)
    grad_queries, grad_keys, grad_values = attend_grad(
        grouping(grad_merged), queries, key_rows, value_rows, log_total, allowed
    )
    grad_packed = jnp.stack([merging(grad_queries), merging(grad_keys), merging(grad_values)])
    grad_wqkv = input_weight_grad(
        normed, grad_packed, "cfpd,kcfpe->kde", jnp.zeros(w_qkv.shape, jnp.float32)
    )
    grad_normed = scatter_grads(
        jnp.einsum("kcfpe,kde->cfpd", grad_packed, w_qkv, preferred_element_type=jnp.float32)
    )
    _, norm_pullback = jax.vjp(layer_norm, residual, norm_gain, norm_bias)
    grad_res, grad_gain, grad_bias = norm_pullback(grad_normed)
    return (grad_out + grad_res, (grad_gain, grad_bias, grad_wqkv, grad_wout))


def mlp_forward(residual, norm_gain, norm_bias, w_in, w_out):
    normed = layer_norm(residual, norm_gain, norm_bias).astype(jnp.bfloat16)
    gathered = gather_rows(normed)
    hidden = jnp.einsum("cfpd,de->cfpe", gathered, w_in, preferred_element_type=jnp.float32)
    active = gelu_exact(hidden).astype(jnp.bfloat16)
    partial_out = jnp.einsum("cfpe,ed->cfpd", active, w_out, preferred_element_type=jnp.float32)
    return (residual + scatter_rows(partial_out), (normed, gathered, hidden, active))


def mlp_backward(grad_out, residual, norm_gain, norm_bias, w_in, w_out, saved):
    normed, gathered, hidden, active = saved
    grad_branch = gather_grads(grad_out.astype(jnp.bfloat16))
    grad_wout = jnp.einsum("cfpe,cfpd->ed", active, grad_branch, preferred_element_type=jnp.float32)
    grad_active = jnp.einsum(
        "cfpd,ed->cfpe", grad_branch, w_out, preferred_element_type=jnp.float32
    )
    _, gelu_pullback = jax.vjp(gelu_exact, hidden)
    grad_hidden = gelu_pullback(grad_active)[0].astype(jnp.bfloat16)
    grad_win = input_weight_grad(
        normed, grad_hidden, "cfpd,cfpe->de", jnp.zeros(w_in.shape, jnp.float32)
    )
    grad_normed = scatter_grads(
        jnp.einsum("cfpe,de->cfpd", grad_hidden, w_in, preferred_element_type=jnp.float32)
    )
    _, norm_pullback = jax.vjp(layer_norm, residual, norm_gain, norm_bias)
    grad_res, grad_gain, grad_bias = norm_pullback(grad_normed)
    return (grad_out + grad_res, (grad_gain, grad_bias, grad_win, grad_wout))


def run_pass(tokens, aspect, cotangent_of, weights):
    (
        gain_one,
        bias_one,
        space_qkv,
        space_out,
        gain_two,
        bias_two,
        time_qkv,
        time_out,
        gain_three,
        bias_three,
        w_in,
        w_out,
    ) = weights
    win_order, win_back = window_maps(aspect, P_SIZE)
    full_shape = (tokens.shape[0], tokens.shape[1], P_SIZE, space_out.shape[0])
    frame_steps = jnp.arange(tokens.shape[1], dtype=jnp.int32)
    allowed = (frame_steps[None, :] <= frame_steps[:, None])[None, None]
    space_group = partial(spatial_groups, win_order)
    space_merge = partial(spatial_merge, win_back, full_shape)
    time_merge = partial(temporal_merge, full_shape)
    block_input = tokens.astype(jnp.float32)
    after_space, space_saved = attention_forward(
        block_input, gain_one, bias_one, space_qkv, space_out, space_group, space_merge, None
    )
    after_time, time_saved = attention_forward(
        after_space, gain_two, bias_two, time_qkv, time_out, temporal_groups, time_merge, allowed
    )
    output, mlp_saved = mlp_forward(after_time, gain_three, bias_three, w_in, w_out)
    grad_output = cotangent_of(output)
    grad_time, mlp_grads = mlp_backward(
        grad_output, after_time, gain_three, bias_three, w_in, w_out, mlp_saved
    )
    grad_space, time_grads = attention_backward(
        grad_time,
        after_space,
        gain_two,
        bias_two,
        time_qkv,
        time_out,
        temporal_groups,
        time_merge,
        allowed,
        time_saved,
    )
    grad_input, space_grads = attention_backward(
        grad_space,
        block_input,
        gain_one,
        bias_one,
        space_qkv,
        space_out,
        space_group,
        space_merge,
        None,
        space_saved,
    )
    return (
        output.astype(jnp.bfloat16),
        grad_input.astype(jnp.bfloat16),
        space_grads + time_grads + mlp_grads,
    )


def shards(
    gen_tokens,
    rec_grad,
    adv_grad,
    gen_aspect,
    gen_frames,
    disc_tokens,
    disc_aspect,
    disc_frames,
    disc_labels,
    logit_gain,
    adv_weight,
    train_step,
    ln1_gain,
    ln1_bias,
    spatial_qkv,
    spatial_out,
    ln2_gain,
    ln2_bias,
    temporal_qkv,
    temporal_out,
    ln3_gain,
    ln3_bias,
    mlp_in,
    mlp_out,
):
    weights = (
        ln1_gain,
        ln1_bias,
        spatial_qkv,
        spatial_out,
        ln2_gain,
        ln2_bias,
        temporal_qkv,
        temporal_out,
        ln3_gain,
        ln3_bias,
        mlp_in,
        mlp_out,
    )
    step_value = train_step[0].astype(jnp.float32)
    ramp = adv_weight[0] * step_value / (step_value + HALF)
    frame_ids = jnp.arange(gen_tokens.shape[1], dtype=jnp.int32)
    gen_live = (frame_ids[None, :] < gen_frames[:, None]).astype(jnp.float32)[:, :, None, None]
    gen_target = gen_live * (rec_grad.astype(jnp.float32) + ramp * adv_grad.astype(jnp.float32))
    disc_live = (frame_ids[None, :] < disc_frames[:, None]).astype(jnp.float32)[:, :, None, None]
    signs = (2 * disc_labels - 1).astype(jnp.float32)[:, None, None, None]

    def gen_cotangent(output):
        return gen_target

    def disc_cotangent(output):
        return -disc_live * signs * logit_gain * jax.nn.sigmoid(1.0 - signs * logit_gain * output)

    gen_out, gen_in_grad, gen_grads = run_pass(gen_tokens, gen_aspect, gen_cotangent, weights)
    disc_out, disc_in_grad, disc_grads = run_pass(disc_tokens, disc_aspect, disc_cotangent, weights)
    split_dims = (0, 0, 1, 1, 0, 0, 1, 1, 0, 0, 0, 1)
    data_count = lax.axis_size("dp")
    reduced = []
    for grad_set in (gen_grads, disc_grads):
        flat, shapes = pack_rows(grad_set, split_dims, data_count)
        flat_sum = lax.psum_scatter(
            flat.astype(jnp.bfloat16), "dp", scatter_dimension=0, tiled=True
        ).astype(jnp.float32)
        reduced.append(unpack_rows(flat_sum, shapes, split_dims, data_count))
    shares = jax.tree.map(jnp.add, tuple(reduced[0]), tuple(reduced[1]))
    norm_shares = lax.psum(
        (shares[0], shares[1], shares[4], shares[5], shares[8], shares[9]), "tensor"
    )
    return (
        gen_out,
        gen_in_grad,
        disc_out,
        disc_in_grad,
        norm_shares[0],
        norm_shares[1],
        shares[2],
        shares[3],
        norm_shares[2],
        norm_shares[3],
        shares[6],
        shares[7],
        norm_shares[4],
        norm_shares[5],
        shares[10],
        shares[11],
    )


def solution(mesh):
    in_specs = (
        P("dp", None, "tensor", None),
        P("dp", None, "tensor", None),
        P("dp", None, "tensor", None),
        P("dp"),
        P("dp"),
        P("dp", None, "tensor", None),
        P("dp"),
        P("dp"),
        P("dp"),
        P(),
        P(),
        P(),
        P(),
        P(),
        P(None, None, "tensor"),
        P("tensor", None),
        P(),
        P(),
        P(None, None, "tensor"),
        P("tensor", None),
        P(),
        P(),
        P(None, "tensor"),
        P("tensor", None),
    )
    out_specs = (
        P("dp", None, "tensor", None),
        P("dp", None, "tensor", None),
        P("dp", None, "tensor", None),
        P("dp", None, "tensor", None),
        P("dp"),
        P("dp"),
        P(None, "dp", "tensor"),
        P("tensor", "dp"),
        P("dp"),
        P("dp"),
        P(None, "dp", "tensor"),
        P("tensor", "dp"),
        P("dp"),
        P("dp"),
        P("dp", "tensor"),
        P("tensor", "dp"),
    )
    return jax.shard_map(shards, mesh=mesh, in_specs=in_specs, out_specs=out_specs, check_vma=False)
```

profile of v0, /device:TPU:0, one launch (start us, length us, event | category | flops | bytes accessed | tf_op | source)
XLA Modules:
  0.0 2304.2 jit_solution(16889734738254080086)
XLA Ops:
  17.4 76.4 %all-gather.25.cloned.1.call-done = bf16[3,5,256,512]{3,2,1,0:T(8,128)(2,1)} async-done(((bf16[3,5,64,512]{3,2,1,0:T(8,128)(2,1)}), bf16[3,5,256,512]{3,2,1,0:T(8,128)(2,1)}) %all-gather.25.cloned.1.call-update) | async-done | bytes 3932176 | tf_op jit(solution)/shard_map/all_gather | solution.py:100
  288.2 67.4 %reduce-scatter.13.cloned.1.call-done = bf16[3,5,64,512]{3,2,1,0:T(8,128)(2,1)} async-done(((bf16[3,5,256,512]{3,2,1,0:T(8,128)(2,1)}), bf16[3,5,64,512]{3,2,1,0:T(8,128)(2,1)}) %reduce-scatter.13.cloned.1.call-update) | async-done | bytes 983056 | tf_op jit(solution)/shard_map/reduce_scatter | solution.py:104
  362.4 76.3 %all-gather.15.cloned.1.call-done = bf16[3,5,256,512]{3,2,1,0:T(8,128)(2,1)} async-done(((bf16[3,5,64,512]{3,2,1,0:T(8,128)(2,1)}), bf16[3,5,256,512]{3,2,1,0:T(8,128)(2,1)}) %all-gather.15.cloned.1.call-update) | async-done | bytes 3932176 | tf_op jit(solution)/shard_map/all_gather | solution.py:100
  454.6 61.2 %all-gather.27.cloned.1.call-done = bf16[3,5,256,512]{3,2,1,0:T(8,128)(2,1)} async-done(((bf16[3,5,64,512]{3,2,1,0:T(8,128)(2,1)}), bf16[3,5,256,512]{3,2,1,0:T(8,128)(2,1)}) %all-gather.27.cloned.1.call-update) | async-done | bytes 3932176 | tf_op jit(solution)/shard_map/all_gather | solution.py:100
  543.4 14.3 fusion.13
  608.4 48.6 %reduce-scatter.27.cloned.1.call-done = bf16[3,5,64,512]{3,2,1,0:T(8,128)(2,1)} async-done(((bf16[3,5,256,512]{3,2,1,0:T(8,128)(2,1)}), bf16[3,5,64,512]{3,2,1,0:T(8,128)(2,1)}) %reduce-scatter.27.cloned.1.call-update) | async-done | bytes 983056 | tf_op jit(solution)/shard_map/reduce_scatter | solution.py:104
  660.3 72.0 %reduce-scatter.15.cloned.1.call-done = bf16[3,5,64,512]{3,2,1,0:T(8,128)(2,1)} async-done(((bf16[3,5,256,512]{3,2,1,0:T(8,128)(2,1)}), bf16[3,5,64,512]{3,2,1,0:T(8,128)(2,1)}) %reduce-scatter.15.cloned.1.call-update) | async-done | bytes 983056 | tf_op jit(solution)/shard_map/reduce_scatter | solution.py:104
  736.7 76.9 %all-gather.29.cloned.1.call-done = bf16[3,5,256,512]{3,2,1,0:T(8,128)(2,1)} async-done(((bf16[3,5,64,512]{3,2,1,0:T(8,128)(2,1)}), bf16[3,5,256,512]{3,2,1,0:T(8,128)(2,1)}) %all-gather.29.cloned.1.call-update) | async-done | bytes 3932176 | tf_op jit(solution)/shard_map/all_gather | solution.py:100
  820.3 18.4 multiply_convert_fusion
  846.4 69.9 %reduce-scatter.29.cloned.1.call-done = bf16[3,5,64,512]{3,2,1,0:T(8,128)(2,1)} async-done(((bf16[3,5,256,512]{3,2,1,0:T(8,128)(2,1)}), bf16[3,5,64,512]{3,2,1,0:T(8,128)(2,1)}) %reduce-scatter.29.cloned.1.call-update) | async-done | bytes 983056 | tf_op jit(solution)/shard_map/reduce_scatter | solution.py:104
  925.4 70.6 %all-gather.31.cloned.1.call-done = bf16[3,5,256,512]{3,2,1,0:T(8,128)(2,1)} async-done(((bf16[3,5,64,512]{3,2,1,0:T(8,128)(2,1)}), bf16[3,5,256,512]{3,2,1,0:T(8,128)(2,1)}) %all-gather.31.cloned.1.call-update) | async-done | bytes 3932176 | tf_op jit(solution)/shard_map/all_gather | solution.py:110
  1014.1 58.9 %all-gather.17.cloned.1.call-done = bf16[3,5,256,512]{3,2,1,0:T(8,128)(2,1)} async-done(((bf16[3,5,64,512]{3,2,1,0:T(8,128)(2,1)}), bf16[3,5,256,512]{3,2,1,0:T(8,128)(2,1)}) %all-gather.17.cloned.1.call-update) | async-done | bytes 3932176 | tf_op jit(solution)/shard_map/all_gather | solution.py:100
  1082.8 18.6 multiply_convert_fusion.1
  1101.5 48.2 %all-gather.19.cloned.1.call-done = bf16[3,5,256,512]{3,2,1,0:T(8,128)(2,1)} async-done(((bf16[3,5,64,512]{3,2,1,0:T(8,128)(2,1)}), bf16[3,5,256,512]{3,2,1,0:T(8,128)(2,1)}) %all-gather.19.cloned.1.call-update) | async-done | bytes 3932176 | tf_op jit(solution)/shard_map/all_gather | solution.py:110
  1170.9 52.2 %reduce-scatter.31.cloned.1.call-done = bf16[3,5,64,512]{3,2,1,0:T(8,128)(2,1)} async-done(((bf16[3,5,256,512]{3,2,1,0:T(8,128)(2,1)}), bf16[3,5,64,512]{3,2,1,0:T(8,128)(2,1)}) %reduce-scatter.31.cloned.1.call-update) | async-done | bytes 983056 | tf_op jit(solution)/shard_map/reduce_scatter | solution.py:114
  1225.0 73.3 %reduce-scatter.19.cloned.1.call-done = bf16[3,5,64,512]{3,2,1,0:T(8,128)(2,1)} async-done(((bf16[3,5,256,512]{3,2,1,0:T(8,128)(2,1)}), bf16[3,5,64,512]{3,2,1,0:T(8,128)(2,1)}) %reduce-scatter.19.cloned.1.call-update) | async-done | bytes 983056 | tf_op jit(solution)/shard_map/reduce_scatter | solution.py:114
  1306.6 66.9 %reduce-scatter.17.cloned.1.call-done = bf16[3,5,64,512]{3,2,1,0:T(8,128)(2,1)} async-done(((bf16[3,5,256,512]{3,2,1,0:T(8,128)(2,1)}), bf16[3,5,64,512]{3,2,1,0:T(8,128)(2,1)}) %reduce-scatter.17.cloned.1.call-update) | async-done | bytes 983056 | tf_op jit(solution)/shard_map/reduce_scatter | solution.py:104
  1378.7 76.3 %all-gather.21.cloned.1.call-done = bf16[3,5,256,512]{3,2,1,0:T(8,128)(2,1)} async-done(((bf16[3,5,64,512]{3,2,1,0:T(8,128)(2,1)}), bf16[3,5,256,512]{3,2,1,0:T(8,128)(2,1)}) %all-gather.21.cloned.1.call-update) | async-done | bytes 3932176 | tf_op jit(solution)/shard_map/all_gather | solution.py:110
  1462.5 69.0 %all-gather.33.cloned.1.call-done = bf16[3,5,256,512]{3,2,1,0:T(8,128)(2,1)} async-done(((bf16[3,5,64,512]{3,2,1,0:T(8,128)(2,1)}), bf16[3,5,256,512]{3,2,1,0:T(8,128)(2,1)}) %all-gather.33.cloned.1.call-update) | async-done | bytes 3932176 | tf_op jit(solution)/shard_map/all_gather | solution.py:110
  1552.0 15.6 multiply_reduce_fusion
  1646.7 31.8 %reduce-scatter.33.cloned.1.call-done = bf16[3,5,64,512]{3,2,1,0:T(8,128)(2,1)} async-done(((bf16[3,5,256,512]{3,2,1,0:T(8,128)(2,1)}), bf16[3,5,64,512]{3,2,1,0:T(8,128)(2,1)}) %reduce-scatter.33.cloned.1.call-update) | async-done | bytes 983056 | tf_op jit(solution)/shard_map/reduce_scatter | solution.py:114
  1680.6 73.2 %reduce-scatter.21.cloned.1.call-done = bf16[3,5,64,512]{3,2,1,0:T(8,128)(2,1)} async-done(((bf16[3,5,256,512]{3,2,1,0:T(8,128)(2,1)}), bf16[3,5,64,512]{3,2,1,0:T(8,128)(2,1)}) %reduce-scatter.21.cloned.1.call-update) | async-done | bytes 983056 | tf_op jit(solution)/shard_map/reduce_scatter | solution.py:114
  1763.3 76.1 %all-gather.23.cloned.1.call-done = bf16[3,5,256,512]{3,2,1,0:T(8,128)(2,1)} async-done(((bf16[3,5,64,512]{3,2,1,0:T(8,128)(2,1)}), bf16[3,5,256,512]{3,2,1,0:T(8,128)(2,1)}) %all-gather.23.cloned.1.call-update) | async-done | bytes 3932176 | tf_op jit(solution)/shard_map/all_gather | solution.py:110
  2203.8 71.7 %all-reduce.6.cloned.1.call-done = (bf16[8,131456]{1,0:T(8,128)(2,1)}, bf16[8,131456]{1,0:T(8,128)(2,1)}) async-done(((bf16[8,131456]{1,0:T(8,128)(2,1)}, bf16[8,131456]{1,0:T(8,128)(2,1)}), (bf16[8,131456]{1,0:T(8,128)(2,1)}, bf16[8,131456]{1,0:T(8,128)(2,1)})) %all-reduce.6.cloned.1.call-update) | async-done | bytes 4206608
  (714 shorter events, 902.6 us)
Async XLA Ops:
  14.5 174.4 %all-gather.13.cloned.1.call-start = ((), (), s32[]{:S(2)}) async-start(), calls=%async_computation.12 | async-start | bytes 4915200 | tf_op jit(solution)/shard_map/all_gather | solution.py:100
  15.2 269.0 %reduce-scatter.25.cloned.1.call-start = ((), (), s32[]{:S(2)}) async-start(), calls=%async_computation.25 | async-start | bytes 4915200 | tf_op jit(solution)/shard_map/reduce_scatter | solution.py:104
  188.5 167.1 %reduce-scatter.13.cloned.1.call-start = ((), (), s32[]{:S(2)}) async-start(), calls=%async_computation.13 | async-start | bytes 4915200 | tf_op jit(solution)/shard_map/reduce_scatter | solution.py:104
  284.2 154.5 %all-gather.15.cloned.1.call-start = ((), (), s32[]{:S(2)}) async-start(), calls=%async_computation.14 | async-start | bytes 4915200 | tf_op jit(solution)/shard_map/all_gather | solution.py:100
  361.7 154.0 %all-gather.27.cloned.1.call-start = ((), (), s32[]{:S(2)}) async-start(), calls=%async_computation.26 | async-start | bytes 4915200 | tf_op jit(solution)/shard_map/all_gather | solution.py:100
  362.3 294.6 %reduce-scatter.27.cloned.1.call-start = ((), (), s32[]{:S(2)}) async-start(), calls=%async_computation.27 | async-start | bytes 4915200 | tf_op jit(solution)/shard_map/reduce_scatter | solution.py:104
  585.6 146.8 %reduce-scatter.15.cloned.1.call-start = ((), (), s32[]{:S(2)}) async-start(), calls=%async_computation.15 | async-start | bytes 4915200 | tf_op jit(solution)/shard_map/reduce_scatter | solution.py:104
  608.3 205.2 %all-gather.29.cloned.1.call-start = ((), (), s32[]{:S(2)}) async-start(), calls=%async_computation.28 | async-start | bytes 4915200 | tf_op jit(solution)/shard_map/all_gather | solution.py:100
  736.6 179.7 %reduce-scatter.29.cloned.1.call-start = ((), (), s32[]{:S(2)}) async-start(), calls=%async_computation.29 | async-start | bytes 4915200 | tf_op jit(solution)/shard_map/reduce_scatter | solution.py:104
  844.9 151.1 %all-gather.31.cloned.1.call-start = ((), (), s32[]{:S(2)}) async-start(), calls=%async_computation.30 | async-start | bytes 4915200 | tf_op jit(solution)/shard_map/all_gather | solution.py:110
  919.1 154.0 %all-gather.17.cloned.1.call-start = ((), (), s32[]{:S(2)}) async-start(), calls=%async_computation.16 | async-start | bytes 4915200 | tf_op jit(solution)/shard_map/all_gather | solution.py:100
  919.6 230.0 %all-gather.19.cloned.1.call-start = ((), (), s32[]{:S(2)}) async-start(), calls=%async_computation.18 | async-start | bytes 4915200 | tf_op jit(solution)/shard_map/all_gather | solution.py:110
  924.9 298.1 %reduce-scatter.31.cloned.1.call-start = ((), (), s32[]{:S(2)}) async-start(), calls=%async_computation.31 | async-start | bytes 4915200 | tf_op jit(solution)/shard_map/reduce_scatter | solution.py:114
  1013.9 284.4 %reduce-scatter.19.cloned.1.call-start = ((), (), s32[]{:S(2)}) async-start(), calls=%async_computation.19 | async-start | bytes 4915200 | tf_op jit(solution)/shard_map/reduce_scatter | solution.py:114
  1164.5 209.0 %reduce-scatter.17.cloned.1.call-start = ((), (), s32[]{:S(2)}) async-start(), calls=%async_computation.17 | async-start | bytes 4915200 | tf_op jit(solution)/shard_map/reduce_scatter | solution.py:104
  1170.9 284.2 %all-gather.21.cloned.1.call-start = ((), (), s32[]{:S(2)}) async-start(), calls=%async_computation.20 | async-start | bytes 4915200 | tf_op jit(solution)/shard_map/all_gather | solution.py:110
  1378.1 153.4 %all-gather.33.cloned.1.call-start = ((), (), s32[]{:S(2)}) async-start(), calls=%async_computation.32 | async-start | bytes 4915200 | tf_op jit(solution)/shard_map/all_gather | solution.py:110
  1378.6 299.9 %reduce-scatter.33.cloned.1.call-start = ((), (), s32[]{:S(2)}) async-start(), calls=%async_computation.33 | async-start | bytes 4915200 | tf_op jit(solution)/shard_map/reduce_scatter | solution.py:114
  1607.1 146.6 %reduce-scatter.21.cloned.1.call-start = ((), (), s32[]{:S(2)}) async-start(), calls=%async_computation.21 | async-start | bytes 4915200 | tf_op jit(solution)/shard_map/reduce_scatter | solution.py:114
  1646.6 192.8 %all-gather.23.cloned.1.call-start = ((), (), s32[]{:S(2)}) async-start(), calls=%async_computation.22 | async-start | bytes 4915200 | tf_op jit(solution)/shard_map/all_gather | solution.py:110
  1762.5 188.7 %all-gather.35.cloned.1.call-start = ((), (), s32[]{:S(2)}) async-start(), calls=%async_computation.34 | async-start | bytes 4915200 | tf_op jit(solution)/shard_map/all_gather | solution.py:110
  1763.3 382.4 %reduce-scatter.23.cloned.1.call-start = ((), (), s32[]{:S(2)}) async-start(), calls=%async_computation.23 | async-start | bytes 4915200 | tf_op jit(solution)/shard_map/reduce_scatter | solution.py:114
  1951.1 196.7 %reduce-scatter.35.cloned.1.call-start = ((), (), s32[]{:S(2)}) async-start(), calls=%async_computation.35 | async-start | bytes 4915200 | tf_op jit(solution)/shard_map/reduce_scatter | solution.py:114
  2062.7 212.8 %all-reduce.6.cloned.1.call-start = ((), (), s32[]{:S(2)}) async-start(), calls=%async_computation.36 | async-start | bytes 8413184
  (169 other events, 5557.3 us)
Sparse Core Ops, SparseCore 0:
  14.6 79.1 all-gather.24
  95.9 74.9 all-gather.12
  188.6 71.2 reduce-scatter.24
  284.3 71.2 reduce-scatter.12
  361.9 76.7 all-gather.14
  440.7 75.0 all-gather.26
  585.7 71.2 reduce-scatter.26
  659.2 73.0 reduce-scatter.14
  736.7 76.7 all-gather.28
  845.0 71.2 reduce-scatter.28
  919.2 76.7 all-gather.30
  998.0 74.9 all-gather.16
  1074.6 74.9 all-gather.18
  1151.8 71.2 reduce-scatter.30
  1225.2 73.0 reduce-scatter.18
  1300.4 73.0 reduce-scatter.16
  1378.2 76.7 all-gather.20
  1456.4 74.9 all-gather.32
  1607.3 71.2 reduce-scatter.32
  1680.7 73.0 reduce-scatter.20
  1762.6 76.7 all-gather.22
  1841.0 74.9 all-gather.34
  2062.8 71.3 reduce-scatter.34
  2195.1 80.3 all-reduce.5
  (1 shorter events, 71.2 us)
where the time goes:
time: 2320 us; the launch traced here: 2300 us
  waiting for transfers between devices  1320 us (57%)
  local copies, waits for them, and re-layouts  470 us (20%)
  matrix products  302 us (13%)
  other arithmetic  180 us (8%)
    all_gather x6, waiting for transfers between devices, gather_rows(): return lax.all_gather(normed, 'tensor', axis=2, tiled=True)  350 us
    all_gather x6, waiting for transfers between devices, gather_grads(): return lax.all_gather(grad_low, 'tensor', axis=2, tiled=True)  340 us
    reduce_scatter x6, waiting for transfers between devices, scatter_rows(): lax.psum_scatter(partial_out.astype(jnp.bfloat16), 'tensor', scatter_dime...  325 us
    reduce_scatter x6, waiting for transfers between devices, scatter_grads(): lax.psum_scatter(partial_grad.astype(jnp.bfloat16), 'tensor', scatter_dim...  230 us
    gather x22, local copies, waits for them, and re-layouts, reorder(): return jax.vmap(partial(jnp.take, axis=1))(values, order)  130 us
    unnamed x26, waiting for transfers between devices  75 us
    reshape x14, local copies, waits for them, and re-layouts, spatial_groups(): reordered.reshape(-1, WIN * WIN, values.shape[-1] // HEAD_DIM, HEAD_DIM)  66.2 us
    unnamed x361, local copies, waits for them, and re-layouts  59 us
  transfers between devices with their start and end apart: 25, of which 20 were waited for; matrix products, arithmetic and copies ran while one was open for 29% of the time, Pallas kernels for 0%

commit v1 on v0

v1 whole, which is shorter than its diff:
```python
from functools import partial
import math

import jax
import jax.numpy as jnp
from jax import lax
from jax.experimental import pallas as pl
from jax.experimental.pallas import tpu as pltpu
from jax.sharding import PartitionSpec as P

HEAD_DIM = 64
WIN = 8
AREA = WIN * WIN
HALF = 5000
EPS = 1e-05
F32 = jnp.float32
BF16 = jnp.bfloat16
VMEM_LIMIT = 56 * 1024 * 1024

NT = (((1,), (1,)), ((), ()))
TN = (((0,), (0,)), ((), ()))


def dot(lhs, rhs):
    return jnp.dot(lhs, rhs, preferred_element_type=F32)


def dot_nt(lhs, rhs):
    return lax.dot_general(lhs, rhs, NT, preferred_element_type=F32)


def dot_tn(lhs, rhs):
    return lax.dot_general(lhs, rhs, TN, preferred_element_type=F32)


def normalize(value):
    average = jnp.mean(value, axis=-1, keepdims=True)
    centred = value - average
    variance = jnp.mean(centred * centred, axis=-1, keepdims=True)
    scale = lax.rsqrt(variance + EPS)
    return centred * scale, scale


def norm_backward(unit, scale, gain, grad):
    scaled = grad * gain
    inner = scaled - jnp.mean(scaled, axis=-1, keepdims=True)
    return scale * (inner - unit * jnp.mean(scaled * unit, axis=-1, keepdims=True))


def row_sums(values):
    return jnp.sum(values.reshape(-1, 8, values.shape[-1]), axis=0)


def params(cost=None):
    return pltpu.CompilerParams(dimension_semantics=("arbitrary",), vmem_limit_bytes=VMEM_LIMIT)


def whole(shape):
    zeros = (0,) * len(shape)
    return pl.BlockSpec(shape, lambda i: zeros)


def per_clip(shape):
    zeros = (0,) * (len(shape) - 1)
    return pl.BlockSpec((1,) + tuple(shape[1:]), lambda i: (i,) + zeros)


def head_mask(dtype):
    rows = lax.broadcasted_iota(jnp.int32, (256, 256), 0) // HEAD_DIM
    cols = lax.broadcasted_iota(jnp.int32, (256, 256), 1) // HEAD_DIM
    return jnp.where(rows == cols, 1.0, 0.0).astype(dtype)


def spread(values, mask):
    return jnp.concatenate([values] * 4, axis=0) * mask


def pair_product(scores, values, low_lane):
    parts = []
    for c in range(2):
        full = dot_tn(scores[:, c * 128 : (c + 1) * 128], values[:, c * 128 : (c + 1) * 128])
        parts.append(jnp.where(low_lane, full[:64], full[64:]))
    return jnp.concatenate(parts, axis=1)


def join_heads(w_ref, full_ref):
    for t in range(w_ref.shape[0]):
        width = w_ref.shape[3]
        for j in range(3):
            full_ref[j, :, t * width : (t + 1) * width] = w_ref[t, j]


def space_forward_kernel(
    x_ref, gain_ref, bias_ref, w_ref, wo_ref, x1_ref, a_ref, qkv_ref, p_ref, o_ref, wfull_ref
):
    @pl.when(pl.program_id(0) == 0)
    def _():
        join_heads(w_ref, wfull_ref)

    rows = x_ref.shape[1]
    x = x_ref[0].astype(F32)
    unit, _ = normalize(x)
    a_ref[0] = (unit * gain_ref[...] + bias_ref[...]).astype(BF16)
    for j in range(3):
        qkv_ref[0, :, j * 512 : (j + 1) * 512] = dot(a_ref[0], wfull_ref[j]).astype(BF16)
    mask = head_mask(BF16)
    low_lane = lax.broadcasted_iota(jnp.int32, (64, 128), 1) < HEAD_DIM
    for w in range(rows // AREA):
        for g in range(2):
            sl = slice(w * AREA, (w + 1) * AREA)
            q, k, v = (
                qkv_ref[0, sl, j * 512 + g * 256 : j * 512 + (g + 1) * 256] for j in range(3)
            )
            s = dot_nt(k, spread(q, mask)) * 0.125
            e = jnp.exp(s - jnp.max(s, axis=0, keepdims=True))
            p = (e * (1.0 / jnp.sum(e, axis=0, keepdims=True))).astype(BF16)
            p_ref[0, 2 * w + g] = p
            o_ref[0, sl, g * 256 : (g + 1) * 256] = pair_product(p, v, low_lane).astype(BF16)
    x1_ref[0] = x + dot(o_ref[0], wo_ref[...])


def space_forward(x, gain, bias, w, wo):
    clips, rows, width = x.shape
    windows = rows // AREA
    shape = jax.ShapeDtypeStruct
    outs = (
        shape((clips, rows, width), F32),
        shape((clips, rows, width), BF16),
        shape((clips, rows, 3 * width), BF16),
        shape((clips, 2 * windows, AREA, 256), BF16),
        shape((clips, rows, width), BF16),
    )
    return pl.pallas_call(
        space_forward_kernel,
        grid=(clips,),
        in_specs=[per_clip(x.shape), whole(gain.shape), whole(bias.shape), whole(w.shape), whole(wo.shape)],
        out_specs=[per_clip(o.shape) for o in outs],
        out_shape=outs,
        scratch_shapes=[pltpu.VMEM((3, width, width), BF16)],
        compiler_params=params(),
    )(x, gain, bias, w, wo)


def space_backward_kernel(
    dx1_ref, x_ref, gain_ref, w_ref, wo_ref, qkv_ref, p_ref,
    dx0_ref, low_ref, dqkv_ref, dg_ref, db_ref, wfull_ref, do_ref,
):
    @pl.when(pl.program_id(0) == 0)
    def _():
        join_heads(w_ref, wfull_ref)
        dg_ref[...] = jnp.zeros_like(dg_ref)
        db_ref[...] = jnp.zeros_like(db_ref)

    rows = x_ref.shape[1]
    low_ref[0] = dx1_ref[0].astype(BF16)
    do_ref[...] = dot_nt(low_ref[0], wo_ref[...]).astype(BF16)
    mask = head_mask(BF16)
    low_lane = lax.broadcasted_iota(jnp.int32, (64, 128), 1) < HEAD_DIM
    for w in range(rows // AREA):
        for g in range(2):
            sl = slice(w * AREA, (w + 1) * AREA)
            q, k, v = (
                qkv_ref[0, sl, j * 512 + g * 256 : j * 512 + (g + 1) * 256] for j in range(3)
            )
            p = p_ref[0, 2 * w + g]
            dob = spread(do_ref[sl, g * 256 : (g + 1) * 256], mask)
            dv = dot(p, dob)
            dp = dot_nt(v, dob)
            p = p.astype(F32)
            weighted = p * dp
            ds = (weighted - p * jnp.sum(weighted, axis=0, keepdims=True)).astype(BF16)
            dk = dot(ds, spread(q, mask)) * 0.125
            dq = pair_product(ds, k, low_lane) * 0.125
            for j, part in enumerate((dq, dk, dv)):
                dqkv_ref[0, sl, j * 512 + g * 256 : j * 512 + (g + 1) * 256] = part.astype(BF16)
    da = sum(dot_nt(dqkv_ref[0, :, j * 512 : (j + 1) * 512], wfull_ref[j]) for j in range(3))
    unit, scale = normalize(x_ref[0].astype(F32))
    dg_ref[...] += row_sums(da * unit)
    db_ref[...] += row_sums(da)
    dx0_ref[0] = (dx1_ref[0] + norm_backward(unit, scale, gain_ref[...], da)).astype(BF16)


def space_backward(dx1, x, gain, w, wo, qkv, p):
    clips, rows, width = x.shape
    shape = jax.ShapeDtypeStruct
    outs = (
        shape((clips, rows, width), BF16),
        shape((clips, rows, width), BF16),
        shape((clips, rows, 3 * width), BF16),
        shape((8, width), F32),
        shape((8, width), F32),
    )
    return pl.pallas_call(
        space_backward_kernel,
        grid=(clips,),
        in_specs=[per_clip(dx1.shape), per_clip(x.shape), whole(gain.shape), whole(w.shape), whole(wo.shape), per_clip(qkv.shape), per_clip(p.shape)],
        out_specs=[per_clip(o.shape) for o in outs[:3]] + [whole((8, width))] * 2,
        out_shape=outs,
        scratch_shapes=[pltpu.VMEM((3, width, width), BF16), pltpu.VMEM((rows, width), BF16)],
        compiler_params=params(),
    )(dx1, x, gain, w, wo, qkv, p)


def head_select(frame):
    rows = lax.broadcasted_iota(jnp.int32, (512, 128), 0) // HEAD_DIM
    cols = lax.broadcasted_iota(jnp.int32, (512, 128), 1) - 8 * frame
    return jnp.where(rows == cols, 1.0, 0.0).astype(BF16)


def head_expand(frame):
    rows = lax.broadcasted_iota(jnp.int32, (128, 512), 0) - 8 * frame
    cols = lax.broadcasted_iota(jnp.int32, (128, 512), 1) // HEAD_DIM
    return jnp.where(rows == cols, 1.0, 0.0).astype(BF16)


def head_sums(products, selector):
    high = products.astype(BF16)
    rest = (products - high.astype(F32)).astype(BF16)
    return dot(high, selector) + dot(rest, selector)


def time_scores(frames, left, right):
    totals = [None] * frames
    for t in range(frames):
        lhs = left(t).astype(F32)
        stacked = jnp.concatenate([lhs * right(f).astype(F32) for f in range(t + 1)], axis=0)
        sums = head_sums(stacked, head_select(t))
        for f in range(t + 1):
            part = sums[f * AREA : (f + 1) * AREA]
            totals[f] = part if totals[f] is None else totals[f] + part
    return totals


def time_forward_kernel(x_ref, gain_ref, bias_ref, w_ref, wo_ref, x2_ref, a_ref, qkv_ref, p_ref, o_ref, wfull_ref):
    @pl.when(pl.program_id(0) == 0)
    def _():
        join_heads(w_ref, wfull_ref)

    rows = x_ref.shape[1]
    frames = rows // AREA
    x = x_ref[0]
    unit, _ = normalize(x)
    a_ref[0] = (unit * gain_ref[...] + bias_ref[...]).astype(BF16)
    for j in range(3):
        qkv_ref[0, :, j * 512 : (j + 1) * 512] = dot(a_ref[0], wfull_ref[j]).astype(BF16)

    def part(j):
        return lambda f: qkv_ref[0, f * AREA : (f + 1) * AREA, j * 512 : (j + 1) * 512]

    scores = time_scores(frames, part(0), part(1))
    lane = lax.broadcasted_iota(jnp.int32, (AREA, 128), 1)
    scores = [jnp.where(lane >= 8 * f, s * 0.125, -1e30) for f, s in enumerate(scores)]
    top = scores[0]
    for s in scores[1:]:
        top = jnp.maximum(top, s)
    exps = [jnp.exp(s - top) for s in scores]
    inverse = 1.0 / sum(exps)
    probs = [e * inverse for e in exps]
    for f in range(frames):
        p_ref[0, f * AREA : (f + 1) * AREA, :] = probs[f]
    low = [p.astype(BF16) for p in probs]
    values = part(2)
    for t in range(frames):
        wide = dot(jnp.concatenate(low[: t + 1], axis=0), head_expand(t))
        total = None
        for f in range(t + 1):
            term = wide[f * AREA : (f + 1) * AREA] * values(f).astype(F32)
            total = term if total is None else total + term
        o_ref[0, t * AREA : (t + 1) * AREA, :] = total.astype(BF16)
    x2_ref[0] = x + dot(o_ref[0], wo_ref[...])


def time_forward(x, gain, bias, w, wo):
    clips, rows, width = x.shape
    shape = jax.ShapeDtypeStruct
    outs = (
        shape((clips, rows, width), F32),
        shape((clips, rows, width), BF16),
        shape((clips, rows, 3 * width), BF16),
        shape((clips, rows, 128), F32),
        shape((clips, rows, width), BF16),
    )
    return pl.pallas_call(
        time_forward_kernel,
        grid=(clips,),
        in_specs=[per_clip(x.shape), whole(gain.shape), whole(bias.shape), whole(w.shape), whole(wo.shape)],
        out_specs=[per_clip(o.shape) for o in outs],
        out_shape=outs,
        scratch_shapes=[pltpu.VMEM((3, width, width), BF16)],
        compiler_params=params(),
    )(x, gain, bias, w, wo)


def time_backward_kernel(
    dx2_ref, x_ref, gain_ref, w_ref, wo_ref, qkv_ref, p_ref,
    dx1_ref, low_ref, dqkv_ref, dg_ref, db_ref, wfull_ref, do_ref,
):
    @pl.when(pl.program_id(0) == 0)
    def _():
        join_heads(w_ref, wfull_ref)
        dg_ref[...] = jnp.zeros_like(dg_ref)
        db_ref[...] = jnp.zeros_like(db_ref)

    rows = x_ref.shape[1]
    frames = rows // AREA
    low_ref[0] = dx2_ref[0].astype(BF16)
    do_ref[...] = dot_nt(low_ref[0], wo_ref[...]).astype(BF16)

    def part(j):
        return lambda f: qkv_ref[0, f * AREA : (f + 1) * AREA, j * 512 : (j + 1) * 512]

    queries, key_rows, values = part(0), part(1), part(2)

    def grads(t):
        return do_ref[t * AREA : (t + 1) * AREA, :]

    dp = time_scores(frames, grads, values)
    probs = [p_ref[0, f * AREA : (f + 1) * AREA, :] for f in range(frames)]
    inner = sum(p * d for p, d in zip(probs, dp))
    ds = [(p * (d - inner)).astype(BF16) for p, d in zip(probs, dp)]
    low = [p.astype(BF16) for p in probs]
    dk = [None] * frames
    dv = [None] * frames
    for t in range(frames):
        wide = dot(jnp.concatenate(ds[: t + 1] + low[: t + 1], axis=0), head_expand(t))
        q, do = queries(t).astype(F32), grads(t).astype(F32)
        dq = None
        for f in range(t + 1):
            ds_wide = wide[f * AREA : (f + 1) * AREA]
            p_wide = wide[(t + 1 + f) * AREA : (t + 2 + f) * AREA]
            term = ds_wide * key_rows(f).astype(F32)
            dq = term if dq is None else dq + term
            dk[f] = ds_wide * q if dk[f] is None else dk[f] + ds_wide * q
            dv[f] = p_wide * do if dv[f] is None else dv[f] + p_wide * do
        dqkv_ref[0, t * AREA : (t + 1) * AREA, 0:512] = (dq * 0.125).astype(BF16)
    for f in range(frames):
        dqkv_ref[0, f * AREA : (f + 1) * AREA, 512:1024] = (dk[f] * 0.125).astype(BF16)
        dqkv_ref[0, f * AREA : (f + 1) * AREA, 1024:1536] = dv[f].astype(BF16)
    da = sum(dot_nt(dqkv_ref[0, :, j * 512 : (j + 1) * 512], wfull_ref[j]) for j in range(3))
    unit, scale = normalize(x_ref[0])
    dg_ref[...] += row_sums(da * unit)
    db_ref[...] += row_sums(da)
    dx1_ref[0] = dx2_ref[0] + norm_backward(unit, scale, gain_ref[...], da)


def time_backward(dx2, x, gain, w, wo, qkv, p):
    clips, rows, width = x.shape
    shape = jax.ShapeDtypeStruct
    outs = (
        shape((clips, rows, width), F32),
        shape((clips, rows, width), BF16),
        shape((clips, rows, 3 * width), BF16),
        shape((8, width), F32),
        shape((8, width), F32),
    )
    return pl.pallas_call(
        time_backward_kernel,
        grid=(clips,),
        in_specs=[per_clip(dx2.shape), per_clip(x.shape), whole(gain.shape), whole(w.shape), whole(wo.shape), per_clip(qkv.shape), per_clip(p.shape)],
        out_specs=[per_clip(o.shape) for o in outs[:3]] + [whole((8, width))] * 2,
        out_shape=outs,
        scratch_shapes=[pltpu.VMEM((3, width, width), BF16), pltpu.VMEM((rows, width), BF16)],
        compiler_params=params(),
    )(dx2, x, gain, w, wo, qkv, p)


def gelu_parts(h):
    e = jnp.exp(h * h * -0.5)
    t = 1.0 / (1.0 + (0.3275911 * math.sqrt(0.5)) * jnp.abs(h))
    tail = t * (0.127414796 + t * (-0.142248368 + t * (0.7107068705 + t * (-0.7265760135 + t * 0.5307027145)))) * e
    cdf = jnp.where(h >= 0, 1.0 - tail, tail)
    return h * cdf, cdf + h * (e * 0.3989422804014327)


def mlp_kernel(
    disc, sign_ref, count_ref, x_ref, gain_ref, bias_ref, win_ref, wout_ref, extra_ref,
    y_ref, dx_ref, c_ref, u_ref, gb_ref, dh_ref, dg_ref, db_ref, slope_ref,
):
    @pl.when(pl.program_id(0) == 0)
    def _():
        dg_ref[...] = jnp.zeros_like(dg_ref)
        db_ref[...] = jnp.zeros_like(db_ref)

    rows = x_ref.shape[1]
    tiles = win_ref.shape[0]
    x = x_ref[0]
    unit, scale = normalize(x)
    c_ref[0] = (unit * gain_ref[...] + bias_ref[...]).astype(BF16)
    y = x
    span = win_ref.shape[2]
    for j in range(tiles):
        h = dot(c_ref[0], win_ref[j])
        active, slope = gelu_parts(h)
        u_ref[0, :, j * span : (j + 1) * span] = active.astype(BF16)
        slope_ref[:, j * span : (j + 1) * span] = slope.astype(BF16)
        y = y + dot(u_ref[0, :, j * span : (j + 1) * span], wout_ref[j])
    y_ref[0] = y.astype(BF16)
    if disc:
        clip = pl.program_id(0)
        sign = sign_ref[clip]
        frame = lax.broadcasted_iota(jnp.int32, (rows, 1), 0) // AREA
        live = jnp.where(frame < count_ref[clip], -sign, 0.0)
        signed = sign * extra_ref[...]
        dy = live * extra_ref[...] * jax.nn.sigmoid(1.0 - signed * y)
    else:
        dy = extra_ref[0].astype(F32)
    gb_ref[0] = dy.astype(BF16)
    dc = None
    for j in range(tiles):
        du = dot_nt(gb_ref[0], wout_ref[j])
        dh = (du * slope_ref[:, j * span : (j + 1) * span].astype(F32)).astype(BF16)
        dh_ref[0, :, j * span : (j + 1) * span] = dh
        term = dot_nt(dh_ref[0, :, j * span : (j + 1) * span], win_ref[j])
        dc = term if dc is None else dc + term
    dg_ref[...] += row_sums(dc * unit)
    db_ref[...] += row_sums(dc)
    dx_ref[0] = dy + norm_backward(unit, scale, gain_ref[...], dc)


def mlp(disc, sign, count, x, gain, bias, win, wout, extra):
    clips, rows, width = x.shape
    hidden = win.shape[0] * win.shape[2]
    shape = jax.ShapeDtypeStruct
    outs = (
        shape((clips, rows, width), BF16),
        shape((clips, rows, width), F32),
        shape((clips, rows, width), BF16),
        shape((clips, rows, hidden), BF16),
        shape((clips, rows, width), BF16),
        shape((clips, rows, hidden), BF16),
        shape((8, width), F32),
        shape((8, width), F32),
    )
    smem = pl.BlockSpec(memory_space=pltpu.SMEM)
    return pl.pallas_call(
        partial(mlp_kernel, disc),
        grid=(clips,),
        in_specs=[smem, smem, per_clip(x.shape), whole(gain.shape), whole(bias.shape), whole(win.shape), whole(wout.shape),
                  whole(extra.shape) if disc else per_clip(extra.shape)],
        out_specs=[per_clip(o.shape) for o in outs[:6]] + [whole((8, width))] * 2,
        out_shape=outs,
        scratch_shapes=[pltpu.VMEM((rows, hidden), BF16)],
        compiler_params=params(),
    )(sign, count, x, gain, bias, win, wout, extra)


def one_hot(source, count):
    rows = source.shape[0]
    inside = lax.broadcasted_iota(jnp.int32, (rows, count), 0) % 8
    cols = lax.broadcasted_iota(jnp.int32, (rows, count), 1)
    return jnp.where((source >= 0) & (cols == source * 8 + inside), 1.0, 0.0).astype(BF16)


def chunk_ids():
    return lax.broadcasted_iota(jnp.int32, (AREA, 1), 0) // 8


def send_source(aspect, t):
    c = chunk_ids()
    square = jnp.where(c < 4, 2 * c + 1 - t % 2, -1)
    wide = jnp.where(
        c < 2, 4 * c + (t ^ 1), jnp.where(c < 4, -1, jnp.where(c < 6, 4 * (c - 4) + (t ^ 2), 4 * (c - 6) + (t ^ 3)))
    )
    return jnp.where(aspect == 0, square, jnp.where(aspect == 1, wide, -1))


def window_source(aspect, t):
    c = chunk_ids()
    square = jnp.where(c < 4, 2 * c + t % 2, c + 4)
    wide = jnp.where(c < 2, 4 * c + t, jnp.where(c < 4, c + 10, jnp.where(c < 6, c + 4, c + 8)))
    return jnp.where(aspect == 0, square, jnp.where(aspect == 1, wide, c))


def raster_source(aspect, t):
    c = chunk_ids()
    square = c // 2 + jnp.where(c % 2 == t % 2, 0, 8)
    way = (c % 4) ^ t
    wide = c // 4 + jnp.where(way == 0, 0, jnp.where(way == 1, 8, jnp.where(way == 2, 12, 14)))
    return jnp.where(aspect == 0, square, jnp.where(aspect == 1, wide, c))


def write_sends(values, refs):
    for f in range(values.shape[0] // AREA):
        base = f * AREA
        refs[0][0, f * 32 : (f + 1) * 32, :] = values[base + 32 : base + 64]
        refs[1][0, f * 16 : (f + 1) * 16, :] = values[base + 16 : base + 32]
        refs[2][0, f * 16 : (f + 1) * 16, :] = values[base + 48 : base + 64]


def pack_rows(values, select, refs):
    for f in range(values.shape[0] // AREA):
        moved = dot(select, values[f * AREA : (f + 1) * AREA]).astype(BF16)
        refs[0][0, f * 32 : (f + 1) * 32, :] = moved[:32]
        refs[1][0, f * 16 : (f + 1) * 16, :] = moved[32:48]
        refs[2][0, f * 16 : (f + 1) * 16, :] = moved[48:]


def pack_kernel(place_ref, aspect_ref, x_ref, *send_refs):
    select = one_hot(send_source(aspect_ref[pl.program_id(0)], place_ref[0]), AREA)
    pack_rows(x_ref[0], select, send_refs)


def pack_grad_kernel(place_ref, aspect_ref, count_ref, ramp_ref, rec_ref, adv_ref, dy_ref, *send_refs):
    clip = pl.program_id(0)
    frame = lax.broadcasted_iota(jnp.int32, (rec_ref.shape[1], 1), 0) // AREA
    total = rec_ref[0].astype(F32) + ramp_ref[0] * adv_ref[0].astype(F32)
    dy_ref[0] = jnp.where(frame < count_ref[clip], total, 0.0).astype(BF16)
    select = one_hot(send_source(aspect_ref[clip], place_ref[0]), AREA)
    pack_rows(dy_ref[0], select, send_refs)


def join_kernel(source, place_ref, aspect_ref, own_ref, r1_ref, r2_ref, r3_ref, out_ref):
    select = one_hot(source(aspect_ref[pl.program_id(0)], place_ref[0]), 2 * AREA)
    for f in range(out_ref.shape[1] // AREA):
        rows = jnp.concatenate(
            [
                own_ref[0, f * AREA : (f + 1) * AREA, :],
                r1_ref[0, f * 32 : (f + 1) * 32, :],
                r2_ref[0, f * 16 : (f + 1) * 16, :],
                r3_ref[0, f * 16 : (f + 1) * 16, :],
            ],
            axis=0,
        )
        out_ref[0, f * AREA : (f + 1) * AREA, :] = dot(select, rows).astype(BF16)


SMEM = pl.BlockSpec(memory_space=pltpu.SMEM)


def send_shapes(x):
    clips, rows, width = x.shape
    return tuple(jax.ShapeDtypeStruct((clips, rows // part, width), BF16) for part in (2, 4, 4))


def pack(place, aspect, x):
    outs = send_shapes(x)
    return pl.pallas_call(
        pack_kernel,
        grid=(x.shape[0],),
        in_specs=[SMEM, SMEM, per_clip(x.shape)],
        out_specs=[per_clip(o.shape) for o in outs],
        out_shape=outs,
        compiler_params=params(),
    )(place, aspect, x)


def pack_grad(place, aspect, count, ramp, rec, adv):
    outs = (jax.ShapeDtypeStruct(rec.shape, BF16),) + send_shapes(rec)
    return pl.pallas_call(
        pack_grad_kernel,
        grid=(rec.shape[0],),
        in_specs=[SMEM, SMEM, SMEM, SMEM, per_clip(rec.shape), per_clip(adv.shape)],
        out_specs=[per_clip(o.shape) for o in outs],
        out_shape=outs,
        compiler_params=params(),
    )(place, aspect, count, ramp, rec, adv)


def join(source, place, aspect, own, parts):
    return pl.pallas_call(
        partial(join_kernel, source),
        grid=(own.shape[0],),
        in_specs=[SMEM, SMEM, per_clip(own.shape)] + [per_clip(p.shape) for p in parts],
        out_specs=per_clip(own.shape),
        out_shape=jax.ShapeDtypeStruct(own.shape, BF16),
        compiler_params=params(),
    )(place, aspect, own, *parts)


def exchange(parts):
    return tuple(
        lax.ppermute(part, "tensor", [(i, i ^ way) for i in range(4)]) for way, part in zip((1, 2, 3), parts)
    )


def window_maps(aspect, tokens_frame):
    grid_side = math.isqrt(tokens_frame)
    grid_width = jnp.where(
        aspect == 1, 2 * grid_side, jnp.where(aspect == 2, grid_side // 2, grid_side)
    ).astype(jnp.int32)[:, None]
    across = grid_width // WIN
    places = jnp.arange(tokens_frame, dtype=jnp.int32)[None, :]
    window = places // AREA
    inside = places % AREA
    grid_row = window // across * WIN + inside // WIN
    grid_col = window % across * WIN + inside % WIN
    forward_order = grid_row * grid_width + grid_col
    raster_row = places // grid_width
    raster_col = places % grid_width
    back_order = (
        (raster_row // WIN * across + raster_col // WIN) * AREA + raster_row % WIN * WIN + raster_col % WIN
    )
    return (forward_order, back_order)


def reorder(values, order):
    return jax.vmap(partial(jnp.take, axis=1))(values, order)


def pad_clips(values, split):
    return jnp.pad(values, [(0, -values.shape[0] % split)] + [(0, 0)] * (values.ndim - 1))


def gather_window(x, aspect, split):
    whole_x = pad_clips(lax.all_gather(x, "tensor", axis=2, tiled=True), split)
    aspect = pad_clips(aspect, split)
    t = lax.axis_index("tensor")
    clips = aspect.shape[0] // split
    mine = lax.dynamic_slice_in_dim(whole_x, t % split * clips, clips, 0)
    kinds = lax.dynamic_slice_in_dim(aspect, t % split * clips, clips, 0)
    order, _ = window_maps(kinds, whole_x.shape[2])
    return reorder(mine, lax.dynamic_slice_in_dim(order, t // split * AREA, AREA, 1))


def gather_raster(y, aspect, split, patches):
    every = lax.all_gather(y, "tensor", axis=0)
    count, clips, frames, _, width = every.shape
    every = every.reshape(count // split, split, clips, frames, AREA, width)
    every = jnp.transpose(every, (1, 2, 3, 0, 4, 5)).reshape(split * clips, frames, -1, width)
    _, back = window_maps(aspect, every.shape[2])
    t = lax.axis_index("tensor")
    return reorder(every[: aspect.shape[0]], lax.dynamic_slice_in_dim(back, t * patches, patches, 1))


def gather_weight(shard):
    rows = shard.shape[0] // lax.axis_size("dp")
    piece = lax.dynamic_slice_in_dim(shard, lax.axis_index("dp") * rows, rows, 0)
    whole_w = lax.all_gather(piece, ("tensor", "dp"), axis=0, tiled=True)
    return whole_w.reshape((-1,) + shard.shape)


def scatter_grad(grads):
    flat = jnp.concatenate([g.astype(BF16).reshape(g.shape[0], -1) for g in grads], axis=1)
    flat = lax.psum_scatter(flat, "dp", scatter_dimension=0, tiled=True)
    pieces, offset = [], 0
    count = lax.axis_size("tensor")
    for g in grads:
        size = math.prod(g.shape[1:])
        piece = flat[:, offset : offset + size].reshape((flat.shape[0],) + g.shape[1:])
        pieces.append(jnp.moveaxis(piece, 2, 0).reshape(count, flat.shape[0], -1))
        offset += size
    mine = lax.psum_scatter(jnp.concatenate(pieces, axis=2), "tensor", scatter_dimension=0, tiled=True)[0]
    results, offset = [], 0
    for g in grads:
        size = g.shape[1] * g.shape[3]
        results.append(mine[:, offset : offset + size].reshape(-1, g.shape[1], g.shape[3]).astype(F32))
        offset += size
    return results


def product_sum(lefts, rights):
    return sum(
        lax.dot_general(a, b, (((0, 1), (0, 1)), ((), ())), preferred_element_type=F32)
        for a, b in zip(lefts, rights)
    )


def shards(
    gen_tokens, rec_grad, adv_grad, gen_aspect, gen_frames, disc_tokens, disc_aspect, disc_frames, disc_labels,
    logit_gain, adv_weight, train_step, ln1_gain, ln1_bias, spatial_qkv, spatial_out, ln2_gain, ln2_bias,
    temporal_qkv, temporal_out, ln3_gain, ln3_bias, mlp_in, mlp_out,
):
    tensor = lax.axis_size("tensor")
    dp_at, tensor_at = lax.axis_index("dp"), lax.axis_index("tensor")
    local, frames, patches, width = gen_tokens.shape
    windows = patches * tensor // AREA
    direct = tensor == 4 and windows == 4
    split = max(tensor // windows, 1)
    clips = -(-local // split)
    place = tensor_at.astype(jnp.int32)[None]
    vectors = [v.reshape(1, -1) for v in (ln1_gain, ln1_bias, ln2_gain, ln2_bias, ln3_gain, ln3_bias, logit_gain)]
    g1, b1, g2, b2, g3, b3, logit = vectors

    step_value = train_step.astype(F32)
    ramp = adv_weight * step_value / (step_value + HALF)

    def mine(values):
        return lax.dynamic_slice_in_dim(pad_clips(values, split), tensor_at % split * clips, clips, 0)

    counts = (mine(gen_frames), mine(disc_frames))
    signs = (2 * mine(disc_labels) - 1).astype(F32)

    def flat(x):
        return x.reshape(x.shape[0], -1, width)

    def to_window(x, aspect):
        if direct:
            return join(window_source, place, aspect, flat(x), exchange(pack(place, aspect, flat(x))))
        return flat(gather_window(x, aspect, split))

    def to_raster(y, aspect):
        if direct:
            by_frame = y.reshape(clips, frames, AREA, width)
            parts = [by_frame[:, :, a:b].reshape(clips, -1, width) for a, b in ((32, 64), (16, 32), (48, 64))]
            return join(raster_source, place, aspect, y, exchange(parts)).reshape(gen_tokens.shape)
        return gather_raster(y.reshape(clips, frames, AREA, width), aspect, split, patches)

    x_gen = to_window(gen_tokens, gen_aspect)
    space_w = gather_weight(spatial_qkv.reshape(3 * width, -1)).reshape(tensor, 3, width, -1)
    space_wo = gather_weight(spatial_out).reshape(width, width)
    time_w = gather_weight(temporal_qkv.reshape(3 * width, -1)).reshape(tensor, 3, width, -1)
    time_wo = gather_weight(temporal_out).reshape(width, width)
    x_disc = to_window(disc_tokens, disc_aspect)
    if direct:
        dy, *parts = pack_grad(place, gen_aspect, gen_frames, ramp, flat(rec_grad), flat(adv_grad))
        dy = join(window_source, place, gen_aspect, dy, exchange(parts))
    else:
        live = jnp.arange(frames, dtype=jnp.int32)[None, :] < gen_frames[:, None]
        total = rec_grad.astype(F32) + ramp[0] * adv_grad.astype(F32)
        dy = jnp.where(live[:, :, None, None], total, 0.0).astype(BF16)
        dy = flat(gather_window(dy, gen_aspect, split))
    w_in = gather_weight(mlp_in)
    w_out = gather_weight(mlp_out)

    xs = (x_gen, x_disc)
    space = [space_forward(x, g1, b1, space_w, space_wo) for x in xs]
    time = [time_forward(s[0], g2, b2, time_w, time_wo) for s in space]
    ff = [
        mlp(bool(i), signs, counts[i], t[0], g3, b3, w_in, w_out, logit if i else dy) for i, t in enumerate(time)
    ]
    outs = [to_raster(m[0], a) for m, a in zip(ff, (gen_aspect, disc_aspect))]
    grad_in = product_sum([m[2] for m in ff], [m[5] for m in ff])
    grad_out = product_sum([m[4] for m in ff], [m[3] for m in ff])
    tb = [time_backward(m[1], s[0], g2, time_w, time_wo, t[2], t[3]) for m, s, t in zip(ff, space, time)]
    time_grad = product_sum([t[1] for t in time], [b[2] for b in tb])
    time_out_grad = product_sum([b[1] for b in tb], [t[4] for t in time])
    sb = [space_backward(b[0], x, g1, space_w, space_wo, s[2], s[3]) for b, x, s in zip(tb, xs, space)]
    ins = [to_raster(b[0], a) for b, a in zip(sb, (gen_aspect, disc_aspect))]
    space_grad = product_sum([s[1] for s in space], [b[2] for b in sb])
    space_out_grad = product_sum([b[1] for b in sb], [s[4] for s in space])

    hidden = mlp_in.shape[1]
    in_share, out_share = scatter_grad(
        [grad_in.reshape(width, 1, tensor, hidden), grad_out.reshape(width, 1, tensor, hidden)]
    )
    part = width // tensor
    time_share, time_out_share = scatter_grad(
        [time_grad.reshape(width, 3, tensor, part), time_out_grad.reshape(width, 1, tensor, part)]
    )
    space_share, space_out_share = scatter_grad(
        [space_grad.reshape(width, 3, tensor, part), space_out_grad.reshape(width, 1, tensor, part)]
    )

    small = jnp.stack(
        [
            jnp.sum(jnp.concatenate([stage[0][k], stage[1][k]], axis=0), axis=0)
            for stage, k in ((sb, 3), (sb, 4), (tb, 3), (tb, 4), (ff, 6), (ff, 7))
        ]
    )
    small = lax.psum(small, ("dp", "tensor"))
    piece = width // lax.axis_size("dp")
    small = lax.dynamic_slice_in_dim(small, dp_at * piece, piece, 1)

    return (
        outs[0], ins[0], outs[1], ins[1],
        small[0], small[1], jnp.transpose(space_share, (1, 0, 2)), space_out_share[:, 0].T,
        small[2], small[3], jnp.transpose(time_share, (1, 0, 2)), time_out_share[:, 0].T,
        small[4], small[5], in_share[:, 0], out_share[:, 0].T,
    )


def solution(mesh):
    tokens = P("dp", None, "tensor", None)
    vector, clip = P(), P("dp")
    qkv, rows, cols = P(None, None, "tensor"), P("tensor", None), P(None, "tensor")
    in_specs = (
        (tokens,) * 3 + (clip,) * 2 + (tokens,) + (clip,) * 3 + (vector,) * 5
        + (qkv, rows, vector, vector, qkv, rows, vector, vector, cols, rows)
    )
    block = (clip, clip, P(None, "dp", "tensor"), P("tensor", "dp"))
    out_specs = (tokens,) * 4 + block * 2 + (clip, clip, P("dp", "tensor"), P("tensor", "dp"))
    return jax.shard_map(shards, mesh=mesh, in_specs=in_specs, out_specs=out_specs, check_vma=False)
```

time: 2320 us -> 611 us (0.26)
  waiting for transfers between devices: 1320 us -> 127 us
  local copies, waits for them, and re-layouts: 470 us -> 28.7 us
  matrix products: 302 us -> 25.1 us
  Pallas kernels: 0 us -> 184 us
  blocking collectives: 12.2 us -> 176 us
  other arithmetic: 180 us -> 18.3 us
  starting transfers between devices: 2.13 us -> 30.6 us
    all_gather x12 -> x4, waiting for transfers between devices: 690 us -> 37.6 us  [gather_weight(): whole_w = lax.all_gather(piece, ('tensor', 'dp'), axis=0, tiled=True)]
    reduce_scatter x12 -> x6, waiting for transfers between devices: 555 us -> 51.8 us  [the longest x3 41.8 us: scatter_grad(): flat = lax.psum_scatter(flat, 'dp', scatter_dimension=0, tiled=True)]
    dot_general x60 -> x12, matrix products: 302 us -> 25.1 us  [product_sum(): lax.dot_general(a, b, (((0, 1), (0, 1)), ((), ())), preferred_element_typ...]
    pallas_call x0 -> x20, Pallas kernels: none -> 184 us  [the longest x2 40.5 us: mlp(): pl.pallas_call(partial(mlp_kernel, disc), grid=(clips,), in_specs=[smem,...]
    reshape x62 -> x13, local copies, waits for them, and re-layouts: 174 us -> 1.18 us  [the longest x10 0.74 us: scatter_grad(): flat[:, offset:offset + size].reshape((flat.shape[0],) + g.shape[1:])]
    gather x22 -> x0, local copies, waits for them, and re-layouts: 130 us -> none  [reorder(): return jax.vmap(partial(jnp.take, axis=1))(values, order)]
    all_gather x0 -> x2, blocking collectives: none -> 129 us  [gather_weight(): whole_w = lax.all_gather(piece, ('tensor', 'dp'), axis=0, tiled=True)]
    convert_element_type x19 -> x1, other arithmetic: 88.4 us -> 0.51 us  [shards(): signs = (2 * mine(disc_labels) - 1).astype(F32)]
  transfers between devices with their start and end apart: 25 -> 31, of which waited for: 20 -> 6; matrix products, arithmetic and copies ran while one was open for 29% -> 9% of each run, Pallas kernels for 0% -> 15%
where the time goes in v1:
time: 611 us; the launch traced here: 607 us
  Pallas kernels  184 us (30%)
  blocking collectives  176 us (29%)
  waiting for transfers between devices  127 us (21%)
  starting transfers between devices  30.6 us (5%)
  local copies, waits for them, and re-layouts  28.7 us (5%)
  matrix products  25.1 us (4%)
  other arithmetic  18.3 us (3%)
  between operations  16.7 us (3%)
    all_gather x2, blocking collectives, gather_weight(): whole_w = lax.all_gather(piece, ('tensor', 'dp'), axis=0, tiled=True)  129 us
    psum x1, blocking collectives, shards(): small = lax.psum(small, ('dp', 'tensor'))  47.6 us
    reduce_scatter x3, waiting for transfers between devices, scatter_grad(): flat = lax.psum_scatter(flat, 'dp', scatter_dimension=0, tiled=True)  41.8 us
    pallas_call x2, Pallas kernels, mlp(): pl.pallas_call(partial(mlp_kernel, disc), grid=(clips,), in_specs=[smem,...  40.5 us
    ppermute x21, waiting for transfers between devices, exchange(): lax.ppermute(part, 'tensor', [(i, i ^ way) for i in range(4)])  37.9 us
    all_gather x4, waiting for transfers between devices, gather_weight(): whole_w = lax.all_gather(piece, ('tensor', 'dp'), axis=0, tiled=True)  37.6 us
    pallas_call x2, Pallas kernels, space_forward(): pl.pallas_call(space_forward_kernel, grid=(clips,), in_specs=[per_clip(x....  30.9 us
    pallas_call x2, Pallas kernels, space_backward(): pl.pallas_call(space_backward_kernel, grid=(clips,), in_specs=[per_clip(d...  30.9 us
  transfers between devices with their start and end apart: 31, of which 6 were waited for; matrix products, arithmetic and copies ran while one was open for 9% of the time, Pallas kernels for 15%

profile of v1, /device:TPU:0, one launch (start us, length us, event | category | flops | bytes accessed | tf_op | source)
XLA Modules:
  0.0 606.6 jit_solution(17017111489269190799)
XLA Ops:
  15.9 4.0 collective-permute-start.1
  29.6 3.8 shard_map.355
  34.2 65.3 %all_gather.21.wo_ref = bf16[512,512]{1,0:T(8,128)(2,1)} all-gather(bf16[16,512]{1,0:T(8,128)(2,1)S(1)} %constant_dynamic-slice_fusion.3), channel_id=1, replica_groups=mesh['dp'=8,'tensor'=4] {'tensor','dp'}, dimensions={0}, use_global_device_ids=true | all-gather | bytes 540672 | tf_op jit(solution)/shard_map/all_gather | solution.py:628
  105.2 63.3 %all_gather.19.wo_ref = bf16[512,512]{1,0:T(8,128)(2,1)} all-gather(bf16[16,512]{1,0:T(8,128)(2,1)S(1)} %constant_dynamic-slice_fusion.5), channel_id=1, replica_groups=mesh['dp'=8,'tensor'=4] {'tensor','dp'}, dimensions={0}, use_global_device_ids=true | all-gather | bytes 540672 | tf_op jit(solution)/shard_map/all_gather | solution.py:628
  182.1 15.5 %shard_map.364 = (f32[3,320,512]{2,1,0:T(8,128)}, bf16[3,320,512]{2,1,0:T(8,128)(2,1)}, bf16[3,320,1536]{2,1,0:T(8,128)(2,1)}, bf16[3,10,64,256]{3,2,1,0:T(8,128)(2,1)}, bf16[3,320,512]{2,1,0:T(8,128)(2,1)}) custom-call(bf16[3,320,512]{2,1,0:T(8,128)(2,1)} %shard_map.363.x_ref, f32[1,512]{1,0:T(1,128)} %bitcast.209, f32[1,512]{1,0:T(1,128)} %bitcast.217, ...), custom_call_target="tpu_custom_call" | custom-call | tf_op jit(solution)/shard_map/pallas_call | solution.py:133
  197.6 15.5 %shard_map.353 = (f32[3,320,512]{2,1,0:T(8,128)}, bf16[3,320,512]{2,1,0:T(8,128)(2,1)}, bf16[3,320,1536]{2,1,0:T(8,128)(2,1)}, bf16[3,10,64,256]{3,2,1,0:T(8,128)(2,1)}, bf16[3,320,512]{2,1,0:T(8,128)(2,1)}) custom-call(bf16[3,320,512]{2,1,0:T(8,128)(2,1)} %shard_map.352.x_ref, f32[1,512]{1,0:T(1,128)} %bitcast.210, f32[1,512]{1,0:T(1,128)} %bitcast.218, ...), custom_call_target="tpu_custom_call" | custom-call | tf_op jit(solution)/shard_map/pallas_call | solution.py:133
  213.1 10.3 %shard_map.365 = (f32[3,320,512]{2,1,0:T(8,128)}, bf16[3,320,512]{2,1,0:T(8,128)(2,1)}, bf16[3,320,1536]{2,1,0:T(8,128)(2,1)}, f32[3,320,128]{2,1,0:T(8,128)}, bf16[3,320,512]{2,1,0:T(8,128)(2,1)}) custom-call(f32[3,320,512]{2,1,0:T(8,128)} %get-tuple-element.102.x_ref, f32[1,512]{1,0:T(1,128)} %bitcast.213, f32[1,512]{1,0:T(1,128)} %bitcast.219, ...), custom_call_target="tpu_custom_call" | custom-call | tf_op jit(solution)/shard_map/pallas_call | solution.py:283
  223.4 10.3 %shard_map.354 = (f32[3,320,512]{2,1,0:T(8,128)}, bf16[3,320,512]{2,1,0:T(8,128)(2,1)}, bf16[3,320,1536]{2,1,0:T(8,128)(2,1)}, f32[3,320,128]{2,1,0:T(8,128)}, bf16[3,320,512]{2,1,0:T(8,128)(2,1)}) custom-call(f32[3,320,512]{2,1,0:T(8,128)} %get-tuple-element.85.x_ref, f32[1,512]{1,0:T(1,128)} %bitcast.214, f32[1,512]{1,0:T(1,128)} %bitcast.220, ...), custom_call_target="tpu_custom_call" | custom-call | tf_op jit(solution)/shard_map/pallas_call | solution.py:283
  233.8 37.5 %all-gather.11.cloned.1.call-done = bf16[2048,512]{1,0:T(8,128)(2,1)} async-done(((bf16[64,512]{1,0:T(8,128)(2,1)}), bf16[2048,512]{1,0:T(8,128)(2,1)}) %all-gather.11.cloned.1.call-update) | async-done | bytes 2097168 | tf_op jit(solution)/shard_map/all_gather | solution.py:628
  271.3 20.3 %shard_map.357 = (bf16[3,320,512]{2,1,0:T(8,128)(2,1)}, f32[3,320,512]{2,1,0:T(8,128)}, bf16[3,320,512]{2,1,0:T(8,128)(2,1)}, bf16[3,320,2048]{2,1,0:T(8,128)(2,...) custom-call(f32[3]{0:T(128)} %add_convert_fusion.sign_ref, ...), custom_call_target="tpu_custom_call" | custom-call | tf_op jit(solution)/shard_map/pallas_call | solution.py:435
  291.6 20.2 %shard_map.366 = (bf16[3,320,512]{2,1,0:T(8,128)(2,1)}, f32[3,320,512]{2,1,0:T(8,128)}, bf16[3,320,512]{2,1,0:T(8,128)(2,1)}, bf16[3,320,2048]{2,1,0:T(8,128)(2,...) custom-call(f32[3]{0:T(128)} %add_convert_fusion.sign_ref, ...), custom_call_target="tpu_custom_call" | custom-call | tf_op jit(solution)/shard_map/pallas_call | solution.py:435
  311.9 12.1 %shard_map.368 = (f32[3,320,512]{2,1,0:T(8,128)}, bf16[3,320,512]{2,1,0:T(8,128)(2,1)}, bf16[3,320,1536]{2,1,0:T(8,128)(2,1)}, f32[8,512]{1,0:T(8,128)}, f32[8,512]{1,0:T(8,128)}) custom-call(f32[3,320,512]{2,1,0:T(8,128)} %get-tuple-element.105.dx2_ref, f32[3,320,512]{2,1,0:T(8,128)} %get-tuple-element.102.x_ref, f32[1,512]{1,0:T(1,128)} %bitcast.215, ...), custom_call_target="tpu_custom_call" | custom-call | tf_op jit(solution)/shard_map/pallas_call | solution.py:356
  324.0 15.6 %shard_map.369 = (bf16[3,320,512]{2,1,0:T(8,128)(2,1)}, bf16[3,320,512]{2,1,0:T(8,128)(2,1)}, bf16[3,320,1536]{2,1,0:T(8,128)(2,1)}, f32[8,512]{1,0:T(8,128)}, f32[8,512]{1,0:T(8,128)}) custom-call(f32[3,320,512]{2,1,0:T(8,128)} %get-tuple-element.108.dx1_ref, bf16[3,320,512]{2,1,0:T(8,128)(2,1)} %shard_map.363.x_ref, f32[1,512]{1,0:T(1,128)} %bitcast.211, ...), custom_call_target="tpu_custom_call" | custom-call | tf_op jit(solution)/shard_map/pallas_call | solution.py:193
  343.8 12.1 %shard_map.359 = (f32[3,320,512]{2,1,0:T(8,128)}, bf16[3,320,512]{2,1,0:T(8,128)(2,1)}, bf16[3,320,1536]{2,1,0:T(8,128)(2,1)}, f32[8,512]{1,0:T(8,128)}, f32[8,512]{1,0:T(8,128)}) custom-call(f32[3,320,512]{2,1,0:T(8,128)} %get-tuple-element.92.dx2_ref, f32[3,320,512]{2,1,0:T(8,128)} %get-tuple-element.85.x_ref, f32[1,512]{1,0:T(1,128)} %bitcast.216, ...), custom_call_target="tpu_custom_call" | custom-call | tf_op jit(solution)/shard_map/pallas_call | solution.py:356
  355.9 15.3 %shard_map.360 = (bf16[3,320,512]{2,1,0:T(8,128)(2,1)}, bf16[3,320,512]{2,1,0:T(8,128)(2,1)}, bf16[3,320,1536]{2,1,0:T(8,128)(2,1)}, f32[8,512]{1,0:T(8,128)}, f32[8,512]{1,0:T(8,128)}) custom-call(f32[3,320,512]{2,1,0:T(8,128)} %get-tuple-element.95.dx1_ref, bf16[3,320,512]{2,1,0:T(8,128)(2,1)} %shard_map.352.x_ref, f32[1,512]{1,0:T(1,128)} %bitcast.212, ...), custom_call_target="tpu_custom_call" | custom-call | tf_op jit(solution)/shard_map/pallas_call | solution.py:193
  386.9 4.8 fusion.15
  405.2 12.3 %reduce-scatter.7.cloned.1.call-done = bf16[64,2048]{1,0:T(8,128)(2,1)} async-done(((bf16[512,2048]{1,0:T(8,128)(2,1)}), bf16[64,2048]{1,0:T(8,128)(2,1)}) %reduce-scatter.7.cloned.1.call-update) | async-done | bytes 262160 | tf_op jit(solution)/shard_map/reduce_scatter | solution.py:634
  436.6 47.6 %psum.7 = f32[6,512]{1,0:T(8,128)S(1)} all-reduce(f32[6,512]{1,0:T(8,128)S(1)} %stack.2), channel_id=1, replica_groups=mesh['dp'=8,'tensor'=4] {'dp','tensor'}, use_global_device_ids=true, to_apply=%region_12.13 | all-reduce | flops 3072 | bytes 24576 | tf_op jit(solution)/shard_map/psum | solution.py:750
  487.7 29.5 %reduce-scatter.15.cloned.1.call-done = bf16[64,4096]{1,0:T(8,128)(2,1)} async-done(((bf16[512,4096]{1,0:T(8,128)(2,1)}), bf16[64,4096]{1,0:T(8,128)(2,1)}) %reduce-scatter.15.cloned.1.call-update) | async-done | bytes 524304 | tf_op jit(solution)/shard_map/reduce_scatter | solution.py:634
  523.3 12.6 %collective-permute-done.16.r2_ref = bf16[3,80,512]{2,1,0:T(8,128)(2,1)S(1)} collective-permute-done((bf16[3,80,512]{2,1,0:T(8,128)(2,1)}, bf16[3,80,512]{2,1,0:T(8,128)(2,1)S(1)}, u32[]{:S(2)}, u32[]{:S(2)}) %collective-permute-start.16) | collective-permute-done | bytes 245792 | tf_op jit(solution)/shard_map/ppermute | solution.py:572
  535.9 3.7 collective-permute-start.20
  548.7 25.3 %collective-permute-done.17.r3_ref = bf16[3,80,512]{2,1,0:T(8,128)(2,1)} collective-permute-done((bf16[3,80,512]{2,1,0:T(8,128)(2,1)S(1)}, bf16[3,80,512]{2,1,0:T(8,128)(2,1)}, u32[]{:S(2)}, u32[]{:S(2)}) %collective-permute-start.17) | collective-permute-done | bytes 245792 | tf_op jit(solution)/shard_map/ppermute | solution.py:572
  574.0 3.8 shard_map.367
  587.9 10.0 %reduce-scatter.17.cloned.1.call-done = bf16[1,64,1024]{2,1,0:T(8,128)(2,1)} async-done(((bf16[4,64,1024]{2,1,0:T(8,128)(2,1)}), bf16[1,64,1024]{2,1,0:T(8,128)(2,1)}) %reduce-scatter.17.cloned.1.call-update) | async-done | bytes 131088 | tf_op jit(solution)/shard_map/reduce_scatter | solution.py:642
  (256 shorter events, 119.1 us)
Async XLA Ops:
  7.2 174.9 %all-gather.5.cloned.1.call-start = ((), (), s32[]{:S(2)}) async-start(), calls=%async_computation.6 | async-start | bytes 1622016 | tf_op jit(solution)/shard_map/all_gather | solution.py:628
  8.8 204.3 %all-gather.7.cloned.1.call-start = ((), (), s32[]{:S(2)}) async-start(), calls=%async_computation.7 | async-start | bytes 1622016 | tf_op jit(solution)/shard_map/all_gather | solution.py:628
  10.3 223.5 %all-gather.9.cloned.1.call-start = ((), (), s32[]{:S(2)}) async-start(), calls=%async_computation.8 | async-start | bytes 2162688 | tf_op jit(solution)/shard_map/all_gather | solution.py:628
  11.0 260.3 %all-gather.11.cloned.1.call-start = ((), (), s32[]{:S(2)}) async-start(), calls=%async_computation.9 | async-start | bytes 2162688 | tf_op jit(solution)/shard_map/all_gather | solution.py:628
  12.5 404.9 %reduce-scatter.7.cloned.1.call-start = ((), (), s32[]{:S(2)}) async-start(), calls=%async_computation.10 | async-start | bytes 2359296 | tf_op jit(solution)/shard_map/reduce_scatter | solution.py:634
  15.9 83.6 %collective-permute-start.1 = (bf16[3,80,512]{2,1,0:T(8,128)(2,1)}, bf16[3,80,512]{2,1,0:T(8,128)(2,1)S(1)}, u32[]{:S(2)}, u32[]{:S(2)}) collective-permute-start(bf16[3,80,512]{2,1,0:T(8,128)(2,1)} %get-tuple-element.83), channel_id=1, source_target_pairs={{0,2},{1,3},{2,0},{3,1},{4,6},{5,7},{6,4},{7,5},{8,10},{9,11},{10,... | collective-permute-start | bytes 737288 | tf_op jit(solution)/shard_map/ppermute | solution.py:572
  19.9 80.9 %collective-permute-start.2 = (bf16[3,80,512]{2,1,0:T(8,128)(2,1)}, bf16[3,80,512]{2,1,0:T(8,128)(2,1)S(1)}, u32[]{:S(2)}, u32[]{:S(2)}) collective-permute-start(bf16[3,80,512]{2,1,0:T(8,128)(2,1)} %get-tuple-element.84), channel_id=1, source_target_pairs={{0,3},{1,2},{2,1},{3,0},{4,7},{5,6},{6,5},{7,4},{8,11},{9,10},{10,... | collective-permute-start | bytes 737288 | tf_op jit(solution)/shard_map/ppermute | solution.py:572
  21.3 83.0 %collective-permute-start = (bf16[3,160,512]{2,1,0:T(8,128)(2,1)}, bf16[3,160,512]{2,1,0:T(8,128)(2,1)S(1)}, u32[]{:S(2)}, u32[]{:S(2)}) collective-permute-start(bf16[3,160,512]{2,1,0:T(8,128)(2,1)} %get-tuple-element.82), channel_id=1, source_target_pairs={{0,1},{1,0},{2,3},{3,2},{4,5},{5,4},{6,7},{7,6},{8,9},{9,8},{10,11... | collective-permute-start | bytes 1474568 | tf_op jit(solution)/shard_map/ppermute | solution.py:572
  24.8 76.0 %collective-permute-start.13 = (bf16[3,80,512]{2,1,0:T(8,128)(2,1)}, bf16[3,80,512]{2,1,0:T(8,128)(2,1)S(1)}, u32[]{:S(2)}, u32[]{:S(2)}) collective-permute-start(bf16[3,80,512]{2,1,0:T(8,128)(2,1)} %get-tuple-element.100), channel_id=1, source_target_pairs={{0,2},{1,3},{2,0},{3,1},{4,6},{5,7},{6,4},{7,5},{8,10},{9,11},{10,... | collective-permute-start | bytes 737288 | tf_op jit(solution)/shard_map/ppermute | solution.py:572
  27.6 144.7 %collective-permute-start.12 = (bf16[3,160,512]{2,1,0:T(8,128)(2,1)}, bf16[3,160,512]{2,1,0:T(8,128)(2,1)S(1)}, u32[]{:S(2)}, u32[]{:S(2)}) collective-permute-start(bf16[3,160,512]{2,1,0:T(8,128)(2,1)} %get-tuple-element.99), channel_id=1, source_target_pairs={{0,1},{1,0},{2,3},{3,2},{4,5},{5,4},{6,7},{7,6},{8,9},{9,8},{10,11... | collective-permute-start | bytes 1474568 | tf_op jit(solution)/shard_map/ppermute | solution.py:572
  99.5 78.0 %collective-permute-start.3 = (bf16[3,160,512]{2,1,0:T(8,128)(2,1)}, bf16[3,160,512]{2,1,0:T(8,128)(2,1)S(1)}, u32[]{:S(2)}, u32[]{:S(2)}) collective-permute-start(bf16[3,160,512]{2,1,0:T(8,128)(2,1)} %get-tuple-element.88), channel_id=1, source_target_pairs={{0,1},{1,0},{2,3},{3,2},{4,5},{5,4},{6,7},{7,6},{8,9},{9,8},{10,11... | collective-permute-start | bytes 1474568 | tf_op jit(solution)/shard_map/ppermute | solution.py:572
  100.8 71.5 %collective-permute-start.14 = (bf16[3,80,512]{2,1,0:T(8,128)(2,1)}, bf16[3,80,512]{2,1,0:T(8,128)(2,1)S(1)}, u32[]{:S(2)}, u32[]{:S(2)}) collective-permute-start(bf16[3,80,512]{2,1,0:T(8,128)(2,1)} %get-tuple-element.101), channel_id=1, source_target_pairs={{0,3},{1,2},{2,1},{3,0},{4,7},{5,6},{6,5},{7,4},{8,11},{9,10},{10,... | collective-permute-start | bytes 737288 | tf_op jit(solution)/shard_map/ppermute | solution.py:572
  100.8 76.6 %collective-permute-start.4 = (bf16[3,80,512]{2,1,0:T(8,128)(2,1)}, bf16[3,80,512]{2,1,0:T(8,128)(2,1)S(1)}, u32[]{:S(2)}, u32[]{:S(2)}) collective-permute-start(bf16[3,80,512]{2,1,0:T(8,128)(2,1)} %get-tuple-element.89), channel_id=1, source_target_pairs={{0,2},{1,3},{2,0},{3,1},{4,6},{5,7},{6,4},{7,5},{8,10},{9,11},{10,... | collective-permute-start | bytes 737288 | tf_op jit(solution)/shard_map/ppermute | solution.py:572
  104.3 73.2 %collective-permute-start.5 = (bf16[3,80,512]{2,1,0:T(8,128)(2,1)}, bf16[3,80,512]{2,1,0:T(8,128)(2,1)S(1)}, u32[]{:S(2)}, u32[]{:S(2)}) collective-permute-start(bf16[3,80,512]{2,1,0:T(8,128)(2,1)} %get-tuple-element.90), channel_id=1, source_target_pairs={{0,3},{1,2},{2,1},{3,0},{4,7},{5,6},{6,5},{7,4},{8,11},{9,10},{10,... | collective-permute-start | bytes 737288 | tf_op jit(solution)/shard_map/ppermute | solution.py:572
  377.2 107.1 %reduce-scatter.11.cloned.1.call-start = ((), (), s32[]{:S(2)}) async-start(), calls=%async_computation.12 | async-start | bytes 2359296 | tf_op jit(solution)/shard_map/reduce_scatter | solution.py:634
  386.6 130.6 %reduce-scatter.15.cloned.1.call-start = ((), (), s32[]{:S(2)}) async-start(), calls=%async_computation.14 | async-start | bytes 4718592 | tf_op jit(solution)/shard_map/reduce_scatter | solution.py:634
  401.5 180.8 %reduce-scatter.9.cloned.1.call-start = ((), (), s32[]{:S(2)}) async-start(), calls=%async_computation.11 | async-start | bytes 327680 | tf_op jit(solution)/shard_map/reduce_scatter | solution.py:642
  403.6 83.9 %collective-permute-start.10 = (bf16[3,80,512]{2,1,0:T(8,128)(2,1)}, bf16[3,80,512]{2,1,0:T(8,128)(2,1)}, u32[]{:S(2)}, u32[]{:S(2)}) collective-permute-start(bf16[3,80,512]{2,1,0:T(8,128)(2,1)} %bitcast.23), channel_id=1, source_target_pairs={{0,2},{1,3},{2,0},{3,1},{4,6},{5,7},{6,4},{7,5},{8,10},{9,11},{10,... | collective-permute-start | bytes 737288 | tf_op jit(solution)/shard_map/ppermute | solution.py:572
  420.4 163.4 %reduce-scatter.13.cloned.1.call-start = ((), (), s32[]{:S(2)}) async-start(), calls=%async_computation.13 | async-start | bytes 327680 | tf_op jit(solution)/shard_map/reduce_scatter | solution.py:642
  428.7 89.9 %collective-permute-start.11 = (bf16[3,80,512]{2,1,0:T(8,128)(2,1)}, bf16[3,80,512]{2,1,0:T(8,128)(2,1)}, u32[]{:S(2)}, u32[]{:S(2)}) collective-permute-start(bf16[3,80,512]{2,1,0:T(8,128)(2,1)} %bitcast.202), channel_id=1, source_target_pairs={{0,3},{1,2},{2,1},{3,0},{4,7},{5,6},{6,5},{7,4},{8,11},{9,10},{10,... | collective-permute-start | bytes 737288 | tf_op jit(solution)/shard_map/ppermute | solution.py:572
  432.1 89.0 %collective-permute-start.7 = (bf16[3,80,512]{2,1,0:T(8,128)(2,1)}, bf16[3,80,512]{2,1,0:T(8,128)(2,1)}, u32[]{:S(2)}, u32[]{:S(2)}) collective-permute-start(bf16[3,80,512]{2,1,0:T(8,128)(2,1)} %bitcast.201), channel_id=1, source_target_pairs={{0,2},{1,3},{2,0},{3,1},{4,6},{5,7},{6,4},{7,5},{8,10},{9,11},{10,... | collective-permute-start | bytes 737288 | tf_op jit(solution)/shard_map/ppermute | solution.py:572
  432.2 90.5 %collective-permute-start.8 = (bf16[3,80,512]{2,1,0:T(8,128)(2,1)}, bf16[3,80,512]{2,1,0:T(8,128)(2,1)}, u32[]{:S(2)}, u32[]{:S(2)}) collective-permute-start(bf16[3,80,512]{2,1,0:T(8,128)(2,1)} %bitcast.200), channel_id=1, source_target_pairs={{0,3},{1,2},{2,1},{3,0},{4,7},{5,6},{6,5},{7,4},{8,11},{9,10},{10,... | collective-permute-start | bytes 737288 | tf_op jit(solution)/shard_map/ppermute | solution.py:572
  434.1 101.7 %collective-permute-start.6 = (bf16[3,160,512]{2,1,0:T(8,128)(2,1)}, bf16[3,160,512]{2,1,0:T(8,128)(2,1)S(1)}, u32[]{:S(2)}, u32[]{:S(2)}) collective-permute-start(bf16[3,160,512]{2,1,0:T(8,128)(2,1)} %bitcast.17), channel_id=1, source_target_pairs={{0,1},{1,0},{2,3},{3,2},{4,5},{5,4},{6,7},{7,6},{8,9},{9,8},{10,11... | collective-permute-start | bytes 1474568 | tf_op jit(solution)/shard_map/ppermute | solution.py:572
  487.3 110.6 %reduce-scatter.17.cloned.1.call-start = ((), (), s32[]{:S(2)}) async-start(), calls=%async_computation.15 | async-start | bytes 655360 | tf_op jit(solution)/shard_map/reduce_scatter | solution.py:642
  (59 other events, 1188.9 us)
Sparse Core Ops, SparseCore 0:
  11.5 67.8 all-gather.4
  82.9 71.1 all-gather.6
  157.5 55.2 all-gather.8
  216.0 55.2 all-gather.10
  377.3 40.1 reduce-scatter.6
  420.9 41.5 reduce-scatter.10
  465.8 51.3 reduce-scatter.14
  519.5 23.6 reduce-scatter.8
  545.5 29.1 reduce-scatter.12
  576.9 20.9 reduce-scatter.16
